TPU v7x, 32 devices: a whole 2x2x4 slice. The times are simulated.
32 devices in a mesh: gx: 4 (over z), gz: 8 (over y, x, core).
Axes of the slice: x: 2, y: 2, z: 4, core: 2. Of those that a mesh axis runs over, the one named last changes fastest.
Arguments:
- velocity: float32 [3, 4096, 1, 4096], P(None, 'gx', None, 'gz'), may hold values from -6 to 6
Outputs:
- advection: float32 [3, 4096, 1, 4096], P(None, 'gx', None, 'gz')
All inputs are finite; a program needn't handle non-finite values.
Results may differ from a plain program's by a relative error of at most 0.00013.
Values sent between devices are 32-bit elements; how exact they have to be, the bound alone decides.
No kernel may reach another device: no remote copies, remote signals or barrier semaphores. Data moves between devices by JAX's collectives and lax.ppermute only.
A program may use at most 128 MiB of HBM per device.

v0:
```python
import functools

import numpy as np
import jax
import jax.numpy as jnp
from jax import lax
from jax.experimental import pallas as pl
from jax.experimental.pallas import tpu as pltpu
from jax.sharding import PartitionSpec as P

ALPHA_D = 1.0 / 3.0
COEF_A = 14.0 / 9.0
COEF_B = 1.0 / 9.0
ALPHA_F = 0.49
block_len = 128

LANES = 128
SUBLANES = 8
REACH_D = 24
REACH_F = 96
RIM = 128
PIECES = 8

ROOT_D = (-1.0 + np.sqrt(1.0 - 4.0 * ALPHA_D**2)) / (2.0 * ALPHA_D)
NEAR_D = COEF_B / (4.0 * ALPHA_D)
GAIN_D = (COEF_A / 2.0 - NEAR_D) * (1.0 - ROOT_D**2) / np.sqrt(1.0 - 4.0 * ALPHA_D**2)
BETA = NEAR_D / GAIN_D


def filter_coefficients():
    return (
        (11.0 + 10.0 * ALPHA_F) / 16.0,
        (15.0 + 34.0 * ALPHA_F) / 32.0,
        (-3.0 + 6.0 * ALPHA_F) / 16.0,
        (1.0 - 2.0 * ALPHA_F) / 32.0,
    )


def split_filter():
    a0, a1, a2, a3 = filter_coefficients()
    poly = [a0 - a2, 0.5 * a1 - 1.5 * a3, 0.5 * a2, 0.5 * a3]
    tap2 = poly[3] / ALPHA_F
    tap1 = (poly[2] - tap2) / ALPHA_F
    tap0 = (poly[1] - tap1) / ALPHA_F
    rest = poly[0] - tap0
    root = (-1.0 + np.sqrt(1.0 - 4.0 * ALPHA_F**2)) / (2.0 * ALPHA_F)
    gain = rest / np.sqrt(1.0 - 4.0 * ALPHA_F**2)
    return root, gain, (tap0 + 2.0 * tap2) / gain, tap1 / gain, tap2 / gain


ROOT_F, GAIN_F, TAP0, TAP1, TAP2 = (float(v) for v in split_filter())
ROOT_D, GAIN_D, BETA = float(ROOT_D), float(GAIN_D), float(BETA)
SCALE = -0.5 * GAIN_D * GAIN_F


def line_table():
    lane = np.arange(LANES)

    def kernel(offset):
        size = np.abs(offset)
        return np.sign(offset) * (ROOT_D ** (np.maximum(size, 1) - 1.0) + BETA * (size == 1))

    inside = kernel(lane[:, None] - lane[None, :])
    source = np.where(lane < LANES // 2, lane + LANES, lane - LANES)
    beside = kernel(source[:, None] - lane[None, :])
    return (SCALE * np.concatenate([inside, beside], axis=0)).astype(np.float32)


def end_table():
    lane = np.arange(LANES)
    table = np.zeros((LANES, LANES))
    tail = LANES - 2.0 - lane
    table[:, 0] = np.where((lane >= LANES // 2) & (lane < LANES - 1), ROOT_D ** np.maximum(tail, 0.0), 0.0)
    table[LANES - 1, 1] = 1.0
    table[0, 2] = 1.0
    table[:, 3] = np.where((lane < LANES // 2) & (lane > 0), ROOT_D ** np.maximum(lane - 1.0, 0.0), 0.0)
    return table.astype(np.float32)


def split_value(value):
    high = value.astype(jnp.bfloat16)
    low = (value - high.astype(jnp.float32)).astype(jnp.bfloat16)
    return high, low


def low_rows():
    return lax.broadcasted_iota(jnp.int32, (SUBLANES, LANES), 0) < SUBLANES // 2


def low_lanes(rows):
    return lax.broadcasted_iota(jnp.int32, (rows, LANES), 1) < LANES // 2


def six_fields(factor, parts):
    return list(parts) + [factor * part for part in parts]


def ends_kernel(seg, v_ref, table_ref, vel_ref, numbers_ref, table, weights, sems, sem):
    rows = LANES
    count = seg // rows

    def load(b):
        at = pl.ds(b * rows, rows)
        return [
            pltpu.make_async_copy(v_ref.at[c, h, at], vel_ref.at[c, at, pl.ds(4 * h, 4)], sems.at[b, 2 * c + h])
            for c in range(3)
            for h in range(2)
        ]

    for b in range(count):
        for copy in load(b):
            copy.start()
        if b == 0:
            fetch = pltpu.make_async_copy(table_ref, table, sem)
            fetch.start()
    fetch.wait()
    for field in range(6):
        moved = table[...] if field == 0 else pltpu.roll(table[...], 4 * field, axis=1)
        high, low = split_value(moved)
        for part in range(2):
            at = pl.ds((2 * field + part) * LANES, LANES)
            weights[at, 0:LANES] = high
            weights[at, LANES:] = low
    flat = vel_ref.reshape(3 * seg * SUBLANES, LANES)
    low_lane = low_lanes(2 * rows)

    for b in range(count):
        for copy in load(b):
            copy.wait()
        parts = []
        for c in range(3):
            chunk = []
            for n in (0, 3):
                chunk.append(
                    jnp.concatenate(
                        [
                            flat[pl.ds((c * seg + b * rows + 8 * k) * SUBLANES + 4 * h + n, 8, stride=SUBLANES), :]
                            for h in range(2)
                            for k in range(rows // 8)
                        ],
                        axis=0,
                    )
                )
            parts.append(jnp.where(low_lane, chunk[0], chunk[1]))
        pieces = []
        for field in six_fields(parts[2], parts):
            pieces += list(split_value(field))
        both = jnp.dot(jnp.concatenate(pieces, axis=1), weights[...], preferred_element_type=jnp.float32)
        numbers = both[:, :LANES] + both[:, LANES:]
        for h in range(2):
            turned = numbers[h * rows : (h + 1) * rows].T
            numbers_ref[:, pl.ds(h * seg + b * rows, rows)] = turned[0:24]


HBM = pl.BlockSpec(memory_space=pl.ANY)
VMEM = pl.BlockSpec(memory_space=pltpu.VMEM)


def ends(view, seg):
    zs = jax.ShapeDtypeStruct((24, 2 * seg), jnp.float32)
    return pl.pallas_call(
        functools.partial(ends_kernel, seg),
        out_shape=(jax.ShapeDtypeStruct((3, seg, SUBLANES, LANES), jnp.float32), zs),
        in_specs=[HBM, HBM],
        out_specs=(VMEM,) * 2,
        scratch_shapes=[
            pltpu.VMEM((LANES, LANES), jnp.float32),
            pltpu.VMEM((12 * LANES, 2 * LANES), jnp.bfloat16),
            pltpu.SemaphoreType.DMA((seg // LANES, 6)),
            pltpu.SemaphoreType.DMA,
        ],
        compiler_params=pltpu.CompilerParams(vmem_limit_bytes=44 * 2**20),
        name="line_ends",
    )(view, jnp.asarray(end_table()))


def x_kernel(seg, vel_ref, s_ref, sums_ref):
    reach = REACH_D
    first = low_rows()
    zero = jnp.zeros((SUBLANES, LANES), jnp.float32)
    start = ((zero,) * 6, (zero,) * 4)

    def advance(values, carry):
        sums, near = carry
        speed = SCALE * values[0]
        terms = six_fields(speed, values)
        bend = BETA * (near[3] + speed)
        found = [(sums[3 + c] + speed * sums[c]) + near[c] * bend for c in range(3)]
        return found, (tuple(term + ROOT_D * total for term, total in zip(terms, sums)), (*values, speed))

    def row(i):
        return [vel_ref[c, i] for c in range(3)]

    def other(i, keep_first):
        turned = [pltpu.roll(value, 4, axis=0) for value in row(i)]
        return [jnp.where(first, value, 0.0) if keep_first else jnp.where(first, 0.0, value) for value in turned]

    def forward(i, carry):
        found, carry = advance(row(i), carry)
        for c in range(3):
            s_ref[c, i] = found[c]
        return carry

    def backward(k, carry):
        i = seg - 1 - k
        found, carry = advance(row(i), carry)
        for c in range(3):
            s_ref[c, i] = found[c] - s_ref[c, i]
        return carry

    carry = lax.fori_loop(0, reach, lambda i, k: advance(other(seg - reach + i, False), k)[1], start, unroll=8)
    carry = lax.fori_loop(0, seg, forward, carry, unroll=8)
    for field in range(6):
        sums_ref[0, field] = carry[0][field]
    carry = lax.fori_loop(0, reach, lambda i, k: advance(other(reach - 1 - i, True), k)[1], start, unroll=8)
    carry = lax.fori_loop(0, seg, backward, carry, unroll=8)
    for field in range(6):
        sums_ref[1, field] = carry[0][field]


def x_part(vel, seg):
    points = 3 * 2 * seg * 4 * LANES
    return pl.pallas_call(
        functools.partial(x_kernel, seg),
        out_shape=(
            jax.ShapeDtypeStruct(vel.shape, jnp.float32),
            jax.ShapeDtypeStruct((2, 6, SUBLANES, LANES), jnp.float32),
        ),
        in_specs=[VMEM],
        out_specs=(VMEM, VMEM),
        compiler_params=pltpu.CompilerParams(vmem_limit_bytes=8 * 2**20),
        cost_estimate=pl.CostEstimate(flops=60 * points, bytes_accessed=8 * points, transcendentals=0),
        name="x_slopes",
    )(vel)


def z_kernel(
    seg, vel_ref, sx_ref, xsums_ref, table_ref, zl_ref, zr_ref,
    o_ref, rim_ref, one_ref, two_ref,
    weights, sbuf, mbuf, turn, halo_hi, halo_lo, pack, sems,
):
    far = REACH_F
    size = seg // PIECES
    step_rows = 32
    pad = step_rows
    total = seg + pad
    rows = 2 * step_rows
    first = low_rows()
    flat = vel_ref.reshape(3 * seg * SUBLANES, LANES)

    for part in range(2):
        high, low = split_value(table_ref[part * LANES : (part + 1) * LANES, :])
        for copy in range(2):
            at = pl.ds((2 * part + copy) * LANES, LANES)
            weights[at, 0:LANES] = high
            weights[at, LANES:] = low

    lane = lax.broadcasted_iota(jnp.int32, (LANES, LANES), 1)
    outer_lane = (lane >= LANES - 2) | (lane < 2)
    from_before = lax.broadcasted_iota(jnp.int32, (24, LANES), 0) % 4 < 2
    turn[24:, :] = jnp.zeros((LANES - 24, LANES), jnp.float32)
    for part in range(2 * seg // LANES):
        at = pl.ds(part * LANES, LANES)
        turn[0:24, :] = jnp.where(from_before, zl_ref[:, at], zr_ref[:, at])
        numbers = turn[...].T
        for field in range(6):
            moved = pltpu.roll(numbers, LANES - 2 - 4 * field, axis=1)
            high, low = split_value(jnp.where(outer_lane, moved, 0.0))
            halo_hi[field, at, :] = high
            halo_lo[field, at, :] = low

    low_lane = low_lanes(rows)

    def s_at(c, row):
        return pl.ds(pl.multiple_of((c * total + pad + row) * SUBLANES, SUBLANES), SUBLANES)

    def strided(c, xi, n):
        return jnp.concatenate(
            [
                flat[pl.ds((c * seg + xi + 8 * k) * SUBLANES + 4 * h + n, 8, stride=SUBLANES), :]
                for h in range(2)
                for k in range(step_rows // 8)
            ],
            axis=0,
        )

    def build(step):
        store = {}
        xi = pl.multiple_of(step * step_rows, step_rows)
        along = [[strided(c, xi, n) for c in range(3)] for n in range(4)]
        for field in range(6):
            halves = []
            for n in range(4):
                value = along[n][field % 3]
                halves.append(split_value(along[n][2] * value if field >= 3 else value))
            for which, halo in ((0, halo_hi), (1, halo_lo)):
                outer = jnp.concatenate(
                    [halo[field, pl.ds(pl.multiple_of(h * seg + xi, 16), step_rows), :] for h in range(2)], axis=0
                )
                line = [outer] + [pair[which] for pair in halves] + [outer]
                for n in range(4):
                    at = pl.ds(((field % 3 * 4 + n) * 2 + field // 3) * rows, rows)
                    store[(field % 3 * 4 + n) * 2 + field // 3, which] = line[n + 1]
                    store[(field % 3 * 4 + n) * 2 + field // 3, 2 + which] = jnp.where(low_lane, line[n + 2], line[n])
        return jnp.concatenate([jnp.concatenate([store[q, p] for p in range(4)], axis=1) for q in range(24)], axis=0)

    def finish(step, both):
        xi = pl.multiple_of(step * step_rows, step_rows)
        alongs = [strided(2, xi, n) for n in range(4)]
        for c in range(3):
            for n in range(4):
                along = alongs[n]
                base = (c * 4 + n) * 2 * rows
                plain = both[base : base + rows]
                mixed = both[base + rows : base + 2 * rows]
                term = (mixed[:, :LANES] + mixed[:, LANES:]) + along * (plain[:, :LANES] + plain[:, LANES:])
                for h in range(2):
                    for k in range(step_rows // 8):
                        at = (c * total + pad + xi + 8 * k) * SUBLANES + 4 * h + n
                        piece = h * (step_rows // 8) + k
                        sbuf[pl.ds(at, 8, stride=SUBLANES), :] = term[piece * 8 : piece * 8 + 8]

    zero = jnp.zeros((SUBLANES, LANES), jnp.float32)

    def row_of(c, row):
        return sbuf[s_at(c, row), :]

    def sweep_row(row, here, carry):
        out = []
        for c in range(3):
            down, scaled1, scaled2, one, two, three, four = carry[c]
            scaled = ROOT_F * down
            taps = TAP0 * two + TAP1 * (one + three) + TAP2 * (here[c] + four)
            mbuf[c, pad + row] = scaled2 + taps
            out.append((here[c] + scaled, scaled, scaled1, here[c], one, two, three))
        return tuple(out)

    def sweep(step, carry):
        for k in range(step_rows):
            row = step * step_rows + k
            here = []
            for c in range(3):
                here.append(row_of(c, row) + sx_ref[c, jnp.maximum(row, 0)])
                sbuf[s_at(c, row), :] = here[c]
            carry = sweep_row(row, here, carry)
        return carry

    def slopes(step):
        return jnp.dot(build(step), weights[...], preferred_element_type=jnp.float32)

    steps = seg // step_rows
    for c in range(3):
        sbuf[pl.ds(c * total * SUBLANES, pad * SUBLANES), :] = jnp.zeros((pad * SUBLANES, LANES), jnp.float32)
    fresh = ((zero,) * 7,) * 3

    def block(pair, carry):
        both = slopes(2 * pair)
        carry = sweep(2 * pair - 1, carry)
        carry = jax.tree.map(lambda value: jnp.where(pair > 0, value, 0.0), carry)
        finish(2 * pair, both)
        both = slopes(2 * pair + 1)
        carry = sweep(2 * pair, carry)
        finish(2 * pair + 1, both)
        return carry

    carry = lax.fori_loop(0, steps // 2, block, fresh)
    carry = sweep(steps - 1, carry)
    down = [carry[c][0] for c in range(3)]
    for k in range(2):
        carry = sweep_row(seg + k, (zero,) * 3, carry)

    low_end = [[pltpu.roll(row_of(c, seg - 1 - k), 4, axis=0) for k in range(2)] for c in range(3)]
    high_start = [[pltpu.roll(row_of(c, k), 4, axis=0) for k in range(2)] for c in range(3)]
    inward = [jnp.where(first, 0.0, pltpu.roll(value, 4, axis=0)) for value in down]

    def carry_over(k, carry):
        out = []
        for c in range(3):
            value = ROOT_F * carry[c]
            mbuf[c, pad + 2 + k] = mbuf[c, pad + 2 + k] + value
            out.append(value)
        return tuple(out)

    lax.fori_loop(0, far, carry_over, tuple(inward), unroll=8)
    for c in range(3):
        begin, end = low_end[c], high_start[c]
        for k, add in ((0, TAP1 * begin[0] + TAP2 * begin[1]), (1, TAP2 * begin[0])):
            mbuf[c, pad + 2 + k] = mbuf[c, pad + 2 + k] + jnp.where(first, 0.0, add)
        for k, add in ((seg - 1, TAP1 * end[0] + TAP2 * end[1]), (seg - 2, TAP2 * end[0])):
            mbuf[c, pad + 2 + k] = mbuf[c, pad + 2 + k] + jnp.where(first, add, 0.0)

    def warm(k, sums):
        return tuple(
            jnp.where(first, pltpu.roll(row_of(c, far - 1 - k), 4, axis=0), 0.0) + ROOT_F * sums[c] for c in range(3)
        )

    sums = lax.fori_loop(0, far, warm, (zero,) * 3, unroll=8)

    def backward(b):
        def body(i, sums):
            row = b * size + size - 1 - i
            out = []
            for c in range(3):
                up = row_of(c, row) + ROOT_F * sums[c]
                mbuf[c, pad + 2 + row] = up + mbuf[c, pad + 2 + row]
                out.append(up)
            return tuple(out)

        return body

    def store(b):
        at = pl.ds(b * size, size)
        held = pl.ds(pad + 2 + b * size, size)
        edge = RIM // size
        return [
            pltpu.make_async_copy(mbuf.at[c, held, pl.ds(4 * h, 4)], o_ref.at[c, h, at], sems.at[b, 2 * c + h])
            for c in range(3)
            for h in range(2)
            if (b >= edge if h == 0 else b < PIECES - edge)
        ]

    for b in reversed(range(PIECES)):
        sums = lax.fori_loop(0, size, backward(b), sums, unroll=16)
        for copy in store(b):
            copy.start()

    def to_rim(k, _):
        for c in range(3):
            rim_ref[c, k] = jnp.where(first, mbuf[c, pad + 2 + k], mbuf[c, pad + 1 + seg - k])
        return 0

    lax.fori_loop(0, RIM, to_rim, 0, unroll=8)

    for field in range(6):
        pack[field] = jnp.where(first, xsums_ref[1, field], xsums_ref[0, field])
    for c in range(3):
        pack[6 + c] = jnp.where(first, vel_ref[c, 0], vel_ref[c, seg - 1])
        pack[9 + c] = jnp.where(first, sums[c], down[c])
        pack[12 + c] = jnp.where(first, row_of(c, 0), row_of(c, seg - 1))
        pack[15 + c] = jnp.where(first, row_of(c, 1), row_of(c, seg - 2))
    weighted = zero
    for k in reversed(range(REACH_D)):
        weighted = jnp.where(first, vel_ref[0, k], vel_ref[0, seg - 1 - k]) + (ROOT_F * ROOT_D) * weighted
    pack[18] = SCALE * weighted
    pack[19] = SCALE * jnp.where(first, vel_ref[0, 1], vel_ref[0, seg - 2])
    even = lax.axis_index("gx") % 2 == 0
    one_ref[...] = jnp.where(even, pack[:, 4:8, :], pack[:, 0:4, :])
    two_ref[...] = jnp.where(even, pack[:, 0:4, :], pack[:, 4:8, :])
    for b in reversed(range(PIECES)):
        for copy in store(b):
            copy.wait()


def z_part(vel, local, xsums, seg, before_z, after_z):
    side = jax.ShapeDtypeStruct((20, 4, LANES), jnp.float32)
    pad = 32
    return pl.pallas_call(
        functools.partial(z_kernel, seg),
        out_shape=(
            jax.ShapeDtypeStruct((3, 2, seg, 4, LANES), jnp.float32),
            jax.ShapeDtypeStruct((3, RIM, SUBLANES, LANES), jnp.float32),
            side,
            side,
        ),
        in_specs=[VMEM] * 6,
        out_specs=(HBM, VMEM, VMEM, VMEM),
        scratch_shapes=[
            pltpu.VMEM((4 * LANES, 2 * LANES), jnp.bfloat16),
            pltpu.VMEM((3 * (seg + pad) * SUBLANES, LANES), jnp.float32),
            pltpu.VMEM((3, seg + pad + 2, SUBLANES, LANES), jnp.float32),
            pltpu.VMEM((LANES, LANES), jnp.float32),
            pltpu.VMEM((6, 2 * seg, LANES), jnp.bfloat16),
            pltpu.VMEM((6, 2 * seg, LANES), jnp.bfloat16),
            pltpu.VMEM((20, SUBLANES, LANES), jnp.float32),
            pltpu.SemaphoreType.DMA((PIECES, 6)),
        ],
        compiler_params=pltpu.CompilerParams(vmem_limit_bytes=32 * 2**20),
        name="z_slopes_and_filter",
    )(vel, local, xsums, jnp.asarray(line_table()), before_z, after_z)


def rim_kernel(seg, o_in, rim_ref, vel_ref, xsums_ref, one_ref, two_ref, o_ref, edge, top, bottom, sems):
    del o_in
    reach = REACH_D
    first = low_rows()
    sign = jnp.where(first, -1.0, 1.0).astype(jnp.float32)
    even = lax.axis_index("gx") % 2 == 0
    edge[:, 0:4, :] = jnp.where(even, two_ref[...], one_ref[...])
    edge[:, 4:8, :] = jnp.where(even, one_ref[...], two_ref[...])
    own = [jnp.where(first, xsums_ref[1, field], xsums_ref[0, field]) for field in range(6)]
    raw = [jnp.where(first, vel_ref[c, 0], vel_ref[c, seg - 1]) for c in range(3)]
    speeds = [SCALE * jnp.where(first, vel_ref[0, k], vel_ref[0, seg - 1 - k]) for k in range(reach)]
    next_to, second = SCALE * edge[6], edge[19]
    for c in range(3):
        bend = (BETA * raw[c]) * (speeds[0] + next_to)
        close = edge[12 + c] - sign * ((own[3 + c] + next_to * own[c]) + bend)
        further = edge[15 + c] - sign * (ROOT_D * (own[3 + c] + second * own[c]))
        gain = 1.0 / (1.0 - ROOT_F * ROOT_D)
        total = edge[9 + c] - sign * ((gain * own[3 + c] + edge[18] * own[c]) + bend)
        change = [
            (sign * ROOT_D**k) * (edge[3 + c] + speeds[k] * edge[c]) for k in range(reach)
        ]
        change[0] = change[0] + sign * ((BETA * edge[6 + c]) * (next_to + speeds[0]))
        line = [further, close] + change + [jnp.zeros_like(close)] * 4
        ups = [None] * reach
        up = jnp.zeros_like(close)
        for k in reversed(range(reach)):
            up = change[k] + ROOT_F * up
            ups[k] = up
        for k in range(RIM):
            scaled = ROOT_F * total
            found = scaled
            if k < reach + 2:
                here = line[k + 2]
                taps = TAP0 * here + TAP1 * (line[k + 1] + line[k + 3]) + TAP2 * (line[k] + line[k + 4])
                found = found + taps
            if k < reach:
                found = found + ups[k]
                total = change[k] + scaled
            else:
                total = scaled
            fixed = rim_ref[c, k] + found
            top[c, k] = fixed
            bottom[c, RIM - 1 - k] = fixed
        pltpu.make_async_copy(top.at[c, :, pl.ds(0, 4)], o_ref.at[c, 0, pl.ds(0, RIM)], sems.at[c, 0]).start()
        pltpu.make_async_copy(
            bottom.at[c, :, pl.ds(4, 4)], o_ref.at[c, 1, pl.ds(seg - RIM, RIM)], sems.at[c, 1]
        ).start()
    for c in range(3):
        pltpu.make_async_copy(top.at[c, :, pl.ds(0, 4)], o_ref.at[c, 0, pl.ds(0, RIM)], sems.at[c, 0]).wait()
        pltpu.make_async_copy(
            bottom.at[c, :, pl.ds(4, 4)], o_ref.at[c, 1, pl.ds(seg - RIM, RIM)], sems.at[c, 1]
        ).wait()


def rim_part(out, rim, vel, xsums, one, two, seg):
    return pl.pallas_call(
        functools.partial(rim_kernel, seg),
        out_shape=jax.ShapeDtypeStruct(out.shape, jnp.float32),
        in_specs=[HBM] + [VMEM] * 5,
        out_specs=HBM,
        input_output_aliases={0: 0},
        scratch_shapes=[
            pltpu.VMEM((20, SUBLANES, LANES), jnp.float32),
            pltpu.VMEM((3, RIM, SUBLANES, LANES), jnp.float32),
            pltpu.VMEM((3, RIM, SUBLANES, LANES), jnp.float32),
            pltpu.SemaphoreType.DMA((3, 2)),
        ],
        compiler_params=pltpu.CompilerParams(vmem_limit_bytes=16 * 2**20),
        name="rim",
    )(out, rim, vel, xsums, one, two)


def ring(axis):
    count = lax.axis_size(axis)
    forward = [(i, (i + 1) % count) for i in range(count)]
    return forward, [(target, source) for source, target in forward]


def pairs(axis):
    count = lax.axis_size(axis)
    one = [(i, i + 1 if i % 2 == 0 else i - 1) for i in range(count)]
    two = [(i, (i - 1 if i % 2 == 0 else i + 1) % count) for i in range(count)]
    return one, two


def blocked(velocity):
    seg = velocity.shape[1] // 2
    vel, numbers = ends(velocity.reshape(3, 2, seg, 4, LANES), seg)
    forward, backward = ring("gz")
    before_z = lax.ppermute(numbers, "gz", forward)
    after_z = lax.ppermute(numbers, "gz", backward)
    local, xsums = x_part(vel, seg)
    out, rim, one, two = z_part(vel, local, xsums, seg, before_z, after_z)
    first_swap, second_swap = pairs("gx")
    one = lax.ppermute(one, "gx", first_swap)
    two = lax.ppermute(two, "gx", second_swap)
    return rim_part(out, rim, vel, xsums, one, two, seg).reshape(velocity.shape)


def with_halo(block, sides, width):
    for axis, dim in sides:
        count = lax.axis_size(axis)
        forward = [(i, i + 1) for i in range(count - 1)]
        forward.append((count - 1, 0))
        backward = [(target, source) for source, target in forward]
        low = lax.ppermute(
            lax.slice_in_dim(block, block.shape[dim] - width, None, axis=dim), axis, forward
        )
        high = lax.ppermute(lax.slice_in_dim(block, 0, width, axis=dim), axis, backward)
        block = jnp.concatenate([low, block, high], axis=dim)
    return block


def tables(length, alpha):
    lower_diag = jnp.concatenate(
        [jnp.zeros((1,), jnp.float32), jnp.full((length - 1,), alpha, jnp.float32)]
    )
    upper_diag = jnp.concatenate(
        [jnp.full((length - 1,), alpha, jnp.float32), jnp.zeros((1,), jnp.float32)]
    )
    main_diag = jnp.ones((length,), jnp.float32)
    identity = jnp.eye(length, dtype=jnp.float32)
    inverse = lax.linalg.tridiagonal_solve(lower_diag, main_diag, upper_diag, identity)
    left_col = alpha * inverse[:, 0]
    right_col = alpha * inverse[:, length - 1]
    coupling = alpha * inverse[0, 0]
    return (inverse, left_col, right_col, coupling)


def offset_slice(extended, offset, length, direction, base=3):
    return lax.slice_in_dim(extended, base + offset, base + offset + length, axis=direction)


def slope_rhs(extended, length, direction, base=3):
    rhs = (
        COEF_A
        * 0.5
        * (
            offset_slice(extended, 1, length, direction, base)
            - offset_slice(extended, -1, length, direction, base)
        )
    )
    return rhs + COEF_B * 0.25 * (
        offset_slice(extended, 2, length, direction, base)
        - offset_slice(extended, -2, length, direction, base)
    )


def smooth_rhs(extended, length, direction, base=3):
    coefficients = filter_coefficients()
    rhs = coefficients[0] * offset_slice(extended, 0, length, direction, base)
    for offset in range(1, 4):
        rhs = rhs + 0.5 * coefficients[offset] * (
            offset_slice(extended, offset, length, direction, base)
            + offset_slice(extended, -offset, length, direction, base)
        )
    return rhs


def wrap_pad(values, direction):
    length = values.shape[direction]
    return jnp.concatenate(
        [
            lax.slice_in_dim(values, length - 3, length, axis=direction),
            values,
            lax.slice_in_dim(values, 0, 3, axis=direction),
        ],
        axis=direction,
    )


def apply_along(inverse, values, direction):
    rotated = jnp.tensordot(
        inverse, values, axes=([1], [direction]), precision=lax.Precision.HIGHEST
    )
    return jnp.moveaxis(rotated, 0, direction)


def end_values(partial_value, direction):
    length = partial_value.shape[direction]
    first_val = lax.slice_in_dim(partial_value, 0, 1, axis=direction)
    last_val = lax.slice_in_dim(partial_value, length - 1, length, axis=direction)
    return (first_val, last_val)


def corrected(partial_value, prev_last, next_first, table, direction):
    inverse, left_col, right_col, coupling = table
    first_val, last_val = end_values(partial_value, direction)
    factor_inv = 1.0 / (1.0 - coupling * coupling)
    left_value = (prev_last - coupling * first_val) * factor_inv
    right_value = (next_first - coupling * last_val) * factor_inv
    dims_list = [1] * partial_value.ndim
    dims_list[direction] = partial_value.shape[direction]
    return (
        partial_value
        - left_col.reshape(dims_list) * left_value
        - right_col.reshape(dims_list) * right_value
    )


def extend_x(values):
    return with_halo(values, (("gx", 1),), 3)


def solve_x(rhs, table):
    partial_value = apply_along(table[0], rhs, 1)
    first_val, last_val = end_values(partial_value, 1)
    beside = with_halo(jnp.concatenate([first_val, last_val], axis=1), (("gx", 1),), 1)
    return corrected(partial_value, beside[:, 0:1], beside[:, 3:4], table, 1)


def solve_blocks(rhs, table):
    dims_list = rhs.shape
    blocks = rhs.reshape(dims_list[:-1] + (dims_list[-1] // block_len, block_len))
    last_dim = blocks.ndim - 1
    partial_value = apply_along(table[0], blocks, last_dim)
    first_val, last_val = end_values(partial_value, last_dim)
    prev_last = jnp.roll(last_val, 1, axis=last_dim - 1)
    next_first = jnp.roll(first_val, -1, axis=last_dim - 1)
    return corrected(partial_value, prev_last, next_first, table, last_dim).reshape(dims_list)


def whole_z_part(velocity):
    slope_z = tables(block_len, ALPHA_D)
    pencil = lax.all_to_all(velocity, "gz", split_axis=1, concat_axis=3, tiled=True)
    along_z = pencil[2:3]
    fields = jnp.concatenate([pencil, along_z * pencil], axis=0)
    slopes = solve_blocks(slope_rhs(wrap_pad(fields, 3), fields.shape[3], 3), slope_z)
    local_terms = slopes[3:] + along_z * slopes[:3]
    return lax.all_to_all(local_terms, "gz", split_axis=3, concat_axis=1, tiled=True)


def per_device(velocity):
    width_x = velocity.shape[1]
    slope_x = tables(width_x, ALPHA_D)
    smooth_x = tables(width_x, ALPHA_F)
    along_x = velocity[0:1]
    rim_source = jnp.concatenate([velocity, along_x * velocity], axis=0)
    padded = extend_x(rim_source)
    slopes_x = solve_x(slope_rhs(padded, width_x, 1), slope_x)
    x_terms = slopes_x[3:] + along_x * slopes_x[:3]
    z_terms = whole_z_part(velocity)
    combined = 0.5 * (x_terms + z_terms)
    smoothed = solve_x(smooth_rhs(extend_x(combined), width_x, 1), smooth_x)
    return -smoothed


def per_block(velocity):
    _, rows, planes, columns = velocity.shape
    fits = planes == 1 and columns == 4 * LANES and rows % 1024 == 0 and lax.axis_size("gx") % 2 == 0
    return blocked(velocity) if fits else per_device(velocity)


def solution(mesh):
    return jax.shard_map(
        per_block,
        mesh=mesh,
        in_specs=(P(None, "gx", None, "gz"),),
        out_specs=P(None, "gx", None, "gz"),
        check_vma=False,
    )
```

profile of v0, /device:TPU:0, one launch (start us, length us, event | category | flops | bytes accessed | tf_op | source)
XLA Modules:
  0.0 39.3 jit_solution(3260171338521886782)
XLA Ops:
  0.0 0.0 copy-start.1
  0.0 0.8 %copy-done.1 = f32[128,128]{1,0:T(8,128)S(1)} copy-done((f32[128,128]{1,0:T(8,128)S(1)}, f32[128,128]{1,0:T(8,128)}, u32[]{:S(2)}) %copy-start.1) | copy-done | bytes 65560
  0.8 0.0 copy-start
  0.8 4.0 %line_ends.1 = (f32[3,512,8,128]{3,2,1,0:T(8,128)S(1)}, f32[24,1024]{1,0:T(8,128)S(1)}) custom-call(f32[3,2,512,4,128]{4,3,2,1,0:T(4,128)} %bitcast.2, f32[128,128]{1,0:T(8,128)S(1)} %copy-done.1), custom_call_target="tpu_custom_call" | custom-call | tf_op jit(solution)/shard_map/line_ends/pallas_call | solution.py:161
  4.9 3.4 %collective-permute-start.1 = (f32[24,1024]{1,0:T(8,128)S(1)}, f32[24,1024]{1,0:T(8,128)S(1)}, u32[]{:S(2)}, u32[]{:S(2)}) collective-permute-start(f32[24,1024]{1,0:T(8,128)S(1)} %get-tuple-element.16), channel_id=1, source_target_pairs={{1,0},{2,1},{3,2},{4,3},{5,4},{6,5},{7,6},{0,7},{9,8},{10,9},{11,1... | collective-permute-start | bytes 294920 | tf_op jit(solution)/shard_map/ppermute | solution.py:572
  8.2 0.0 collective-permute-start
  8.2 5.4 %x_slopes.1 = (f32[3,512,8,128]{3,2,1,0:T(8,128)S(1)}, f32[2,6,8,128]{3,2,1,0:T(8,128)S(1)}) custom-call(f32[3,512,8,128]{3,2,1,0:T(8,128)S(1)} %get-tuple-element.13.vel_ref), custom_call_target="tpu_custom_call" | custom-call | flops 94371840 | bytes 12582912 | tf_op jit(solution)/shard_map/x_slopes/pallas_call | solution.py:223
  13.7 0.0 collective-permute-done.1.zr_ref
  13.7 0.0 collective-permute-done.zl_ref
  13.7 0.0 copy-done
  13.7 16.7 %z_slopes_and_filter.1 = (f32[3,2,512,4,128]{4,3,2,1,0:T(4,128)}, f32[3,128,8,128]{3,2,1,0:T(8,128)S(1)}, f32[20,4,128]{2,1,0:T(4,128)S(1)}, f32[20,4,128]{2,1,0:T(4,128)S(1)}) custom-call(f32[3,512,8,128]{3,2,1,0:T(8,128)S(1)} %get-tuple-element.13.vel_ref, f32[3,512,8,128]{3,2,1,0:T(8,128)S(1)} %get-tuple-element.14.sx_ref, ...), custom_call_target="tpu_custom_call" | custom-call | tf_op jit(solution)/shard_map/z_slopes_and_filter/pallas_call | solution.py:457
  30.4 1.6 %collective-permute-start.2 = (f32[20,4,128]{2,1,0:T(4,128)S(1)}, f32[20,4,128]{2,1,0:T(4,128)S(1)}, u32[]{:S(2)}, u32[]{:S(2)}) collective-permute-start(f32[20,4,128]{2,1,0:T(4,128)S(1)} %get-tuple-element.19), channel_id=1, source_target_pairs={{0,8},{8,0},{16,24},{24,16},{1,9},{9,1},{17,25},{25,17},{2,10},{10... | collective-permute-start | bytes 122888 | tf_op jit(solution)/shard_map/ppermute | solution.py:576
  32.0 2.5 %collective-permute-start.3 = (f32[20,4,128]{2,1,0:T(4,128)S(1)}, f32[20,4,128]{2,1,0:T(4,128)S(1)}, u32[]{:S(2)}, u32[]{:S(2)}) collective-permute-start(f32[20,4,128]{2,1,0:T(4,128)S(1)} %get-tuple-element.20), channel_id=1, source_target_pairs={{0,24},{8,16},{16,8},{24,0},{1,25},{9,17},{17,9},{25,1},{2,26},{10... | collective-permute-start | bytes 122888 | tf_op jit(solution)/shard_map/ppermute | solution.py:577
  34.5 0.0 collective-permute-done.2.one_ref
  34.5 3.3 %collective-permute-done.3.two_ref = f32[20,4,128]{2,1,0:T(4,128)S(1)} collective-permute-done((f32[20,4,128]{2,1,0:T(4,128)S(1)}, f32[20,4,128]{2,1,0:T(4,128)S(1)}, u32[]{:S(2)}, u32[]{:S(2)}) %collective-permute-start.3) | collective-permute-done | bytes 40992 | tf_op jit(solution)/shard_map/ppermute | solution.py:577
  37.8 1.4 %rim.1 = f32[3,2,512,4,128]{4,3,2,1,0:T(4,128)} custom-call(f32[3,2,512,4,128]{4,3,2,1,0:T(4,128)} %get-tuple-element.17.o_in, f32[3,128,8,128]{3,2,1,0:T(8,128)S(1)} %get-tuple-element.18.rim_ref, f32[3,512,8,128]{3,2,1,0:T(8,128)S(1)} %get-tuple-element.13.vel_ref, ...), custom_call_target="tpu_custom_call", output_to_operand_aliasing={{}: (0, {})} | custom-call | tf_op jit(solution)/shard_map/rim/pallas_call | solution.py:537
Async XLA Ops:
  0.0 0.8 %copy-start.1 = (f32[128,128]{1,0:T(8,128)S(1)}, f32[128,128]{1,0:T(8,128)}, u32[]{:S(2)}) copy-start(f32[128,128]{1,0:T(8,128)} %constant.4.clone.table_ref) | copy-start | bytes 196612
  0.8 12.9 %copy-start = (f32[256,128]{1,0:T(8,128)S(1)}, f32[256,128]{1,0:T(8,128)}, u32[]{:S(2)}) copy-start(f32[256,128]{1,0:T(8,128)} %constant.5.clone.table_ref) | copy-start | bytes 393220
  4.9 8.8 %collective-permute-start.1 = (f32[24,1024]{1,0:T(8,128)S(1)}, f32[24,1024]{1,0:T(8,128)S(1)}, u32[]{:S(2)}, u32[]{:S(2)}) collective-permute-start(f32[24,1024]{1,0:T(8,128)S(1)} %get-tuple-element.16), channel_id=1, source_target_pairs={{1,0},{2,1},{3,2},{4,3},{5,4},{6,5},{7,6},{0,7},{9,8},{10,9},{11,1... | collective-permute-start | bytes 294920 | tf_op jit(solution)/shard_map/ppermute | solution.py:572
  8.2 5.4 %collective-permute-start = (f32[24,1024]{1,0:T(8,128)S(1)}, f32[24,1024]{1,0:T(8,128)S(1)}, u32[]{:S(2)}, u32[]{:S(2)}) collective-permute-start(f32[24,1024]{1,0:T(8,128)S(1)} %get-tuple-element.16), channel_id=1, source_target_pairs={{0,1},{1,2},{2,3},{3,4},{4,5},{5,6},{6,7},{7,0},{8,9},{9,10},{10,1... | collective-permute-start | bytes 294920 | tf_op jit(solution)/shard_map/ppermute | solution.py:571
  30.4 4.1 %collective-permute-start.2 = (f32[20,4,128]{2,1,0:T(4,128)S(1)}, f32[20,4,128]{2,1,0:T(4,128)S(1)}, u32[]{:S(2)}, u32[]{:S(2)}) collective-permute-start(f32[20,4,128]{2,1,0:T(4,128)S(1)} %get-tuple-element.19), channel_id=1, source_target_pairs={{0,8},{8,0},{16,24},{24,16},{1,9},{9,1},{17,25},{25,17},{2,10},{10... | collective-permute-start | bytes 122888 | tf_op jit(solution)/shard_map/ppermute | solution.py:576
  32.0 5.8 %collective-permute-start.3 = (f32[20,4,128]{2,1,0:T(4,128)S(1)}, f32[20,4,128]{2,1,0:T(4,128)S(1)}, u32[]{:S(2)}, u32[]{:S(2)}) collective-permute-start(f32[20,4,128]{2,1,0:T(4,128)S(1)} %get-tuple-element.20), channel_id=1, source_target_pairs={{0,24},{8,16},{16,8},{24,0},{1,25},{9,17},{17,9},{25,1},{2,26},{10... | collective-permute-start | bytes 122888 | tf_op jit(solution)/shard_map/ppermute | solution.py:577
where the time goes:
time: 39.4 us; the launch traced here: 39.3 us
  Pallas kernels  27.5 us (70%)
  starting transfers between devices  7.51 us (19%)
  waiting for transfers between devices  3.33 us (8%)
  local copies, waits for them, and re-layouts  0.84 us (2%)
    pallas_call x1, Pallas kernels, z_part(): pl.pallas_call(functools.partial(z_kernel, seg), out_shape=(jax.ShapeDtyp...  16.7 us
    pallas_call x1, Pallas kernels, x_part(): pl.pallas_call(functools.partial(x_kernel, seg), out_shape=(jax.ShapeDtyp...  5.42 us
    pallas_call x1, Pallas kernels, ends(): pl.pallas_call(functools.partial(ends_kernel, seg), out_shape=(jax.ShapeD...  4.01 us
    ppermute x1, starting transfers between devices, blocked(): after_z = lax.ppermute(numbers, 'gz', backward)  3.39 us
    ppermute x1, waiting for transfers between devices, blocked(): two = lax.ppermute(two, 'gx', second_swap)  3.32 us
    ppermute x1, starting transfers between devices, blocked(): two = lax.ppermute(two, 'gx', second_swap)  2.48 us
    ppermute x1, starting transfers between devices, blocked(): one = lax.ppermute(one, 'gx', first_swap)  1.64 us
    pallas_call x1, Pallas kernels, rim_part(): pl.pallas_call(functools.partial(rim_kernel, seg), out_shape=jax.ShapeDty...  1.41 us
  transfers between devices with their start and end apart: 4, of which 1 were waited for; matrix products, arithmetic and copies ran while one was open for 0% of the time, Pallas kernels for 14%

commit v1 on v0

--- a/solution.py
+++ b/solution.py
@@ -19,7 +19,10 @@
 REACH_D = 24
 REACH_F = 96
 RIM = 128
-PIECES = 8
+STEP_ROWS = 64
+PIECES = 4
+AHEAD = 4
+GROUP = 4
 
 ROOT_D = (-1.0 + np.sqrt(1.0 - 4.0 * ALPHA_D**2)) / (2.0 * ALPHA_D)
 NEAR_D = COEF_B / (4.0 * ALPHA_D)
@@ -67,14 +70,15 @@
 
 
 def end_table():
-    lane = np.arange(LANES)
-    table = np.zeros((LANES, LANES))
-    tail = LANES - 2.0 - lane
-    table[:, 0] = np.where((lane >= LANES // 2) & (lane < LANES - 1), ROOT_D ** np.maximum(tail, 0.0), 0.0)
-    table[LANES - 1, 1] = 1.0
-    table[0, 2] = 1.0
-    table[:, 3] = np.where((lane < LANES // 2) & (lane > 0), ROOT_D ** np.maximum(lane - 1.0, 0.0), 0.0)
-    return table.astype(np.float32)
+    row = lax.broadcasted_iota(jnp.int32, (LANES, LANES), 0)
+    lane = lax.broadcasted_iota(jnp.int32, (LANES, LANES), 1)
+    starts = row < LANES // 2
+    steps = jnp.where(starts, row - 1, LANES - 2 - row)
+    size = jnp.exp(float(np.log(-ROOT_D)) * jnp.maximum(steps, 0).astype(jnp.float32))
+    power = jnp.where(steps % 2 == 0, size, -size)
+    inner = (steps >= 0) & (lane == jnp.where(starts, 3, 0))
+    edge = (steps < 0) & (lane == jnp.where(starts, 2, 1))
+    return jnp.where(inner, power, jnp.where(edge, 1.0, 0.0))
 
 
 def split_value(value):
@@ -95,7 +99,7 @@
     return list(parts) + [factor * part for part in parts]
 
 
-def ends_kernel(seg, v_ref, table_ref, vel_ref, numbers_ref, table, weights, sems, sem):
+def ends_kernel(seg, v_ref, vel_ref, numbers_ref, weights, sems):
     rows = LANES
     count = seg // rows
 
@@ -107,41 +111,40 @@
             for h in range(2)
         ]
 
-    for b in range(count):
+    for b in range(AHEAD):
         for copy in load(b):
             copy.start()
-        if b == 0:
-            fetch = pltpu.make_async_copy(table_ref, table, sem)
-            fetch.start()
-    fetch.wait()
+    table = end_table()
     for field in range(6):
-        moved = table[...] if field == 0 else pltpu.roll(table[...], 4 * field, axis=1)
+        moved = table if field == 0 else pltpu.roll(table, 4 * field, axis=1)
         high, low = split_value(moved)
         for part in range(2):
             at = pl.ds((2 * field + part) * LANES, LANES)
             weights[at, 0:LANES] = high
             weights[at, LANES:] = low
+    low_lane = low_lanes(2 * rows)
     flat = vel_ref.reshape(3 * seg * SUBLANES, LANES)
-    low_lane = low_lanes(2 * rows)
 
     for b in range(count):
         for copy in load(b):
             copy.wait()
+        if b + AHEAD < count:
+            for copy in load(b + AHEAD):
+                copy.start()
         parts = []
         for c in range(3):
-            chunk = []
-            for n in (0, 3):
-                chunk.append(
-                    jnp.concatenate(
-                        [
-                            flat[pl.ds((c * seg + b * rows + 8 * k) * SUBLANES + 4 * h + n, 8, stride=SUBLANES), :]
-                            for h in range(2)
-                            for k in range(rows // 8)
-                        ],
-                        axis=0,
-                    )
+            start, end = (
+                jnp.concatenate(
+                    [
+                        flat[pl.ds((c * seg + b * rows + 8 * k) * SUBLANES + 4 * h + n, 8, stride=SUBLANES), :]
+                        for h in range(2)
+                        for k in range(rows // 8)
+                    ],
+                    axis=0,
                 )
-            parts.append(jnp.where(low_lane, chunk[0], chunk[1]))
+                for n in (0, 3)
+            )
+            parts.append(jnp.where(low_lane, start, end))
         pieces = []
         for field in six_fields(parts[2], parts):
             pieces += list(split_value(field))
@@ -157,21 +160,21 @@
 
 
 def ends(view, seg):
-    zs = jax.ShapeDtypeStruct((24, 2 * seg), jnp.float32)
     return pl.pallas_call(
         functools.partial(ends_kernel, seg),
-        out_shape=(jax.ShapeDtypeStruct((3, seg, SUBLANES, LANES), jnp.float32), zs),
-        in_specs=[HBM, HBM],
-        out_specs=(VMEM,) * 2,
+        out_shape=(
+            jax.ShapeDtypeStruct((3, seg, SUBLANES, LANES), jnp.float32),
+            jax.ShapeDtypeStruct((24, 2 * seg), jnp.float32),
+        ),
+        in_specs=[HBM],
+        out_specs=(VMEM, VMEM),
         scratch_shapes=[
-            pltpu.VMEM((LANES, LANES), jnp.float32),
             pltpu.VMEM((12 * LANES, 2 * LANES), jnp.bfloat16),
             pltpu.SemaphoreType.DMA((seg // LANES, 6)),
-            pltpu.SemaphoreType.DMA,
         ],
         compiler_params=pltpu.CompilerParams(vmem_limit_bytes=44 * 2**20),
         name="line_ends",
-    )(view, jnp.asarray(end_table()))
+    )(view)
 
 
 def x_kernel(seg, vel_ref, s_ref, sums_ref):
@@ -209,11 +212,11 @@
         return carry
 
     carry = lax.fori_loop(0, reach, lambda i, k: advance(other(seg - reach + i, False), k)[1], start, unroll=8)
-    carry = lax.fori_loop(0, seg, forward, carry, unroll=8)
+    carry = lax.fori_loop(0, seg, forward, carry, unroll=16)
     for field in range(6):
         sums_ref[0, field] = carry[0][field]
     carry = lax.fori_loop(0, reach, lambda i, k: advance(other(reach - 1 - i, True), k)[1], start, unroll=8)
-    carry = lax.fori_loop(0, seg, backward, carry, unroll=8)
+    carry = lax.fori_loop(0, seg, backward, carry, unroll=16)
     for field in range(6):
         sums_ref[1, field] = carry[0][field]
 
@@ -228,7 +231,7 @@
         ),
         in_specs=[VMEM],
         out_specs=(VMEM, VMEM),
-        compiler_params=pltpu.CompilerParams(vmem_limit_bytes=8 * 2**20),
+        compiler_params=pltpu.CompilerParams(vmem_limit_bytes=16 * 2**20),
         cost_estimate=pl.CostEstimate(flops=60 * points, bytes_accessed=8 * points, transcendentals=0),
         name="x_slopes",
     )(vel)
@@ -236,14 +239,11 @@
 
 def z_kernel(
     seg, vel_ref, sx_ref, xsums_ref, table_ref, zl_ref, zr_ref,
-    o_ref, rim_ref, one_ref, two_ref,
-    weights, sbuf, mbuf, turn, halo_hi, halo_lo, pack, sems,
+    sbuf, ups_ref, downs_ref, one_ref, two_ref,
+    weights, turn, halo_hi, halo_lo, pack,
 ):
     far = REACH_F
-    size = seg // PIECES
-    step_rows = 32
-    pad = step_rows
-    total = seg + pad
+    step_rows = STEP_ROWS
     rows = 2 * step_rows
     first = low_rows()
     flat = vel_ref.reshape(3 * seg * SUBLANES, LANES)
@@ -269,10 +269,7 @@
             halo_hi[field, at, :] = high
             halo_lo[field, at, :] = low
 
-    low_lane = low_lanes(rows)
-
-    def s_at(c, row):
-        return pl.ds(pl.multiple_of((c * total + pad + row) * SUBLANES, SUBLANES), SUBLANES)
+    low_lane = jnp.where(low_lanes(rows), 1.0, 0.0).astype(jnp.bfloat16) > 0.5
 
     def strided(c, xi, n):
         return jnp.concatenate(
@@ -316,126 +313,38 @@
                 term = (mixed[:, :LANES] + mixed[:, LANES:]) + along * (plain[:, :LANES] + plain[:, LANES:])
                 for h in range(2):
                     for k in range(step_rows // 8):
-                        at = (c * total + pad + xi + 8 * k) * SUBLANES + 4 * h + n
+                        at = (c * seg + xi + 8 * k) * SUBLANES + 4 * h + n
                         piece = h * (step_rows // 8) + k
                         sbuf[pl.ds(at, 8, stride=SUBLANES), :] = term[piece * 8 : piece * 8 + 8]
 
     zero = jnp.zeros((SUBLANES, LANES), jnp.float32)
 
+    def block(step, _):
+        finish(step, jnp.dot(build(step), weights[...], preferred_element_type=jnp.float32))
+        return 0
+
+    lax.fori_loop(0, seg // step_rows, block, 0)
+
     def row_of(c, row):
-        return sbuf[s_at(c, row), :]
-
-    def sweep_row(row, here, carry):
-        out = []
-        for c in range(3):
-            down, scaled1, scaled2, one, two, three, four = carry[c]
-            scaled = ROOT_F * down
-            taps = TAP0 * two + TAP1 * (one + three) + TAP2 * (here[c] + four)
-            mbuf[c, pad + row] = scaled2 + taps
-            out.append((here[c] + scaled, scaled, scaled1, here[c], one, two, three))
-        return tuple(out)
-
-    def sweep(step, carry):
-        for k in range(step_rows):
-            row = step * step_rows + k
-            here = []
-            for c in range(3):
-                here.append(row_of(c, row) + sx_ref[c, jnp.maximum(row, 0)])
-                sbuf[s_at(c, row), :] = here[c]
-            carry = sweep_row(row, here, carry)
-        return carry
-
-    def slopes(step):
-        return jnp.dot(build(step), weights[...], preferred_element_type=jnp.float32)
-
-    steps = seg // step_rows
+        at = pl.ds(pl.multiple_of((c * seg + row) * SUBLANES, SUBLANES), SUBLANES)
+        return sbuf[at, :] + sx_ref[c, row]
+
+    def sums_of(k, sums):
+        ups, downs = sums
+        ups = tuple(row_of(c, far - 1 - k) + ROOT_F * ups[c] for c in range(3))
+        downs = tuple(row_of(c, seg - far + k) + ROOT_F * downs[c] for c in range(3))
+        return ups, downs
+
+    ups, downs = lax.fori_loop(0, far, sums_of, ((zero,) * 3,) * 2, unroll=8)
     for c in range(3):
-        sbuf[pl.ds(c * total * SUBLANES, pad * SUBLANES), :] = jnp.zeros((pad * SUBLANES, LANES), jnp.float32)
-    fresh = ((zero,) * 7,) * 3
-
-    def block(pair, carry):
-        both = slopes(2 * pair)
-        carry = sweep(2 * pair - 1, carry)
-        carry = jax.tree.map(lambda value: jnp.where(pair > 0, value, 0.0), carry)
-        finish(2 * pair, both)
-        both = slopes(2 * pair + 1)
-        carry = sweep(2 * pair, carry)
-        finish(2 * pair + 1, both)
-        return carry
-
-    carry = lax.fori_loop(0, steps // 2, block, fresh)
-    carry = sweep(steps - 1, carry)
-    down = [carry[c][0] for c in range(3)]
-    for k in range(2):
-        carry = sweep_row(seg + k, (zero,) * 3, carry)
-
-    low_end = [[pltpu.roll(row_of(c, seg - 1 - k), 4, axis=0) for k in range(2)] for c in range(3)]
-    high_start = [[pltpu.roll(row_of(c, k), 4, axis=0) for k in range(2)] for c in range(3)]
-    inward = [jnp.where(first, 0.0, pltpu.roll(value, 4, axis=0)) for value in down]
-
-    def carry_over(k, carry):
-        out = []
-        for c in range(3):
-            value = ROOT_F * carry[c]
-            mbuf[c, pad + 2 + k] = mbuf[c, pad + 2 + k] + value
-            out.append(value)
-        return tuple(out)
-
-    lax.fori_loop(0, far, carry_over, tuple(inward), unroll=8)
-    for c in range(3):
-        begin, end = low_end[c], high_start[c]
-        for k, add in ((0, TAP1 * begin[0] + TAP2 * begin[1]), (1, TAP2 * begin[0])):
-            mbuf[c, pad + 2 + k] = mbuf[c, pad + 2 + k] + jnp.where(first, 0.0, add)
-        for k, add in ((seg - 1, TAP1 * end[0] + TAP2 * end[1]), (seg - 2, TAP2 * end[0])):
-            mbuf[c, pad + 2 + k] = mbuf[c, pad + 2 + k] + jnp.where(first, add, 0.0)
-
-    def warm(k, sums):
-        return tuple(
-            jnp.where(first, pltpu.roll(row_of(c, far - 1 - k), 4, axis=0), 0.0) + ROOT_F * sums[c] for c in range(3)
-        )
-
-    sums = lax.fori_loop(0, far, warm, (zero,) * 3, unroll=8)
-
-    def backward(b):
-        def body(i, sums):
-            row = b * size + size - 1 - i
-            out = []
-            for c in range(3):
-                up = row_of(c, row) + ROOT_F * sums[c]
-                mbuf[c, pad + 2 + row] = up + mbuf[c, pad + 2 + row]
-                out.append(up)
-            return tuple(out)
-
-        return body
-
-    def store(b):
-        at = pl.ds(b * size, size)
-        held = pl.ds(pad + 2 + b * size, size)
-        edge = RIM // size
-        return [
-            pltpu.make_async_copy(mbuf.at[c, held, pl.ds(4 * h, 4)], o_ref.at[c, h, at], sems.at[b, 2 * c + h])
-            for c in range(3)
-            for h in range(2)
-            if (b >= edge if h == 0 else b < PIECES - edge)
-        ]
-
-    for b in reversed(range(PIECES)):
-        sums = lax.fori_loop(0, size, backward(b), sums, unroll=16)
-        for copy in store(b):
-            copy.start()
-
-    def to_rim(k, _):
-        for c in range(3):
-            rim_ref[c, k] = jnp.where(first, mbuf[c, pad + 2 + k], mbuf[c, pad + 1 + seg - k])
-        return 0
-
-    lax.fori_loop(0, RIM, to_rim, 0, unroll=8)
+        ups_ref[c] = ups[c]
+        downs_ref[c] = downs[c]
 
     for field in range(6):
         pack[field] = jnp.where(first, xsums_ref[1, field], xsums_ref[0, field])
     for c in range(3):
         pack[6 + c] = jnp.where(first, vel_ref[c, 0], vel_ref[c, seg - 1])
-        pack[9 + c] = jnp.where(first, sums[c], down[c])
+        pack[9 + c] = jnp.where(first, ups[c], downs[c])
         pack[12 + c] = jnp.where(first, row_of(c, 0), row_of(c, seg - 1))
         pack[15 + c] = jnp.where(first, row_of(c, 1), row_of(c, seg - 2))
     weighted = zero
@@ -446,37 +355,188 @@
     even = lax.axis_index("gx") % 2 == 0
     one_ref[...] = jnp.where(even, pack[:, 4:8, :], pack[:, 0:4, :])
     two_ref[...] = jnp.where(even, pack[:, 0:4, :], pack[:, 4:8, :])
-    for b in reversed(range(PIECES)):
-        for copy in store(b):
-            copy.wait()
 
 
 def z_part(vel, local, xsums, seg, before_z, after_z):
     side = jax.ShapeDtypeStruct((20, 4, LANES), jnp.float32)
-    pad = 32
     return pl.pallas_call(
         functools.partial(z_kernel, seg),
         out_shape=(
-            jax.ShapeDtypeStruct((3, 2, seg, 4, LANES), jnp.float32),
-            jax.ShapeDtypeStruct((3, RIM, SUBLANES, LANES), jnp.float32),
+            jax.ShapeDtypeStruct((3 * seg * SUBLANES, LANES), jnp.float32),
+            jax.ShapeDtypeStruct((3, SUBLANES, LANES), jnp.float32),
+            jax.ShapeDtypeStruct((3, SUBLANES, LANES), jnp.float32),
             side,
             side,
         ),
         in_specs=[VMEM] * 6,
-        out_specs=(HBM, VMEM, VMEM, VMEM),
+        out_specs=(VMEM,) * 5,
         scratch_shapes=[
             pltpu.VMEM((4 * LANES, 2 * LANES), jnp.bfloat16),
-            pltpu.VMEM((3 * (seg + pad) * SUBLANES, LANES), jnp.float32),
-            pltpu.VMEM((3, seg + pad + 2, SUBLANES, LANES), jnp.float32),
             pltpu.VMEM((LANES, LANES), jnp.float32),
             pltpu.VMEM((6, 2 * seg, LANES), jnp.bfloat16),
             pltpu.VMEM((6, 2 * seg, LANES), jnp.bfloat16),
             pltpu.VMEM((20, SUBLANES, LANES), jnp.float32),
+        ],
+        compiler_params=pltpu.CompilerParams(vmem_limit_bytes=20 * 2**20),
+        name="z_slopes",
+    )(vel, local, xsums, jnp.asarray(line_table()), before_z, after_z)
+
+
+def filter_kernel(seg, z_ref, x_ref, ups_ref, downs_ref, o_ref, rim_ref, s_buf, o_buf, sems):
+    size = seg // PIECES
+    turns = size // GROUP
+    warm_group = REACH_F // turns
+    first = low_rows()
+
+    def term(c, row):
+        at = pl.ds(pl.multiple_of((c * seg + row) * SUBLANES, SUBLANES), SUBLANES)
+        return z_ref[at, :] + x_ref[c, row]
+
+    def to_second(value):
+        return jnp.where(first, 0.0, pltpu.roll(value, 4, axis=0))
+
+    def to_first(value):
+        return jnp.where(first, pltpu.roll(value, 4, axis=0), 0.0)
+
+    def down_row(here, carry):
+        found, out = [], []
+        for c in range(3):
+            down, scaled1, scaled2, one, two, three, four = carry[c]
+            scaled = ROOT_F * down
+            taps = TAP0 * two + TAP1 * (one + three) + TAP2 * (here[c] + four)
+            found.append(scaled2 + taps)
+            out.append((here[c] + scaled, scaled, scaled1, here[c], one, two, three))
+        return found, tuple(out)
+
+    def down_rows(b, i, carry):
+        low = b * size + 2 + GROUP * i
+        count = GROUP
+        lines = [[term(c, low + k) for c in range(3)] for k in range(count)]
+        results = []
+        for here in lines:
+            found, carry = down_row(here, carry)
+            results.append(found)
+        for k in range(count):
+            for c in range(3):
+                s_buf[c, low + k] = lines[k][c]
+                o_buf[c, low + k - 2] = results[k][c]
+        return carry
+
+    def warm_rows(b, i, ups):
+        top = (b + 1) * size + REACH_F - 1 - warm_group * i
+        lines = [[term(c, top - k) for c in range(3)] for k in range(warm_group)]
+        for here in lines:
+            ups = tuple(here[c] + ROOT_F * ups[c] for c in range(3))
+        return ups
+
+    def up_rows(b, i, ups):
+        low = (b + 1) * size - GROUP * (i + 1)
+        order = list(reversed(range(GROUP)))
+        here = {(k, c): s_buf[c, low + k] for k in order for c in range(3)}
+        found = {(k, c): o_buf[c, low + k] for k in order for c in range(3)}
+        for k in order:
+            ups = tuple(here[k, c] + ROOT_F * ups[c] for c in range(3))
+            for c in range(3):
+                found[k, c] = found[k, c] + ups[c]
+        for k in order:
+            for c in range(3):
+                o_buf[c, low + k] = found[k, c]
+        return ups
+
+    def store(b):
+        at = pl.ds(b * size, size)
+        edge = RIM // size
+        return [
+            pltpu.make_async_copy(o_buf.at[c, at, pl.ds(4 * h, 4)], o_ref.at[c, h, at], sems.at[b, 2 * c + h])
+            for c in range(3)
+            for h in range(2)
+            if (b >= edge if h == 0 else b < PIECES - edge)
+        ]
+
+    zero = jnp.zeros((SUBLANES, LANES), jnp.float32)
+    zeros = (zero,) * 3
+    carry = tuple(
+        (
+            to_second(downs_ref[c]), zero, zero,
+            to_second(term(c, seg - 1)), to_second(term(c, seg - 2)), zero, zero,
+        )
+        for c in range(3)
+    )
+    for k in range(2):
+        here = [term(c, k) for c in range(3)]
+        for c in range(3):
+            s_buf[c, k] = here[c]
+        carry = down_row(here, carry)[1]
+    for c in range(3):
+        for k in range(2):
+            s_buf[c, seg + k] = to_first(s_buf[c, k])
+    last = tuple(to_first(ups_ref[c]) for c in range(3))
+
+    def opening(i, state):
+        carry, warmed = state
+        return down_rows(0, i, carry), warm_rows(0, i, warmed)
+
+    carry, warmed = lax.fori_loop(0, turns, opening, (carry, zeros), unroll=4)
+    for b in range(PIECES):
+        if b < PIECES - 2:
+
+            def body(i, state, b=b):
+                carry, warmed, ups = state
+                return down_rows(b + 1, i, carry), warm_rows(b + 1, i, warmed), up_rows(b, i, ups)
+
+            carry, warmed, _ = lax.fori_loop(0, turns, body, (carry, zeros, warmed), unroll=4)
+        elif b == PIECES - 2:
+
+            def body(i, state, b=b):
+                carry, ups = state
+                return down_rows(b + 1, i, carry), up_rows(b, i, ups)
+
+            carry, _ = lax.fori_loop(0, turns - 1, body, (carry, warmed))
+            _ = up_rows(b, turns - 1, _)
+            low = seg - GROUP + 2
+            for k in range(GROUP):
+                row = low + k
+                here = [term(c, row) if row < seg else s_buf[c, row] for c in range(3)]
+                found, carry = down_row(here, carry)
+                for c in range(3):
+                    if row < seg:
+                        s_buf[c, row] = here[c]
+                    o_buf[c, row - 2] = found[c]
+        else:
+            lax.fori_loop(0, turns, lambda i, ups: up_rows(PIECES - 1, i, ups), last)
+        for copy in store(b):
+            copy.start()
+
+    def to_rim(k, _):
+        for c in range(3):
+            rim_ref[c, k] = jnp.where(first, o_buf[c, k], o_buf[c, seg - 1 - k])
+        return 0
+
+    lax.fori_loop(0, RIM, to_rim, 0, unroll=8)
+    for b in range(PIECES):
+        for copy in store(b):
+            copy.wait()
+
+
+def filter_part(terms, local, ups, downs, seg):
+    points = 3 * 2 * seg * 4 * LANES
+    return pl.pallas_call(
+        functools.partial(filter_kernel, seg),
+        out_shape=(
+            jax.ShapeDtypeStruct((3, 2, seg, 4, LANES), jnp.float32),
+            jax.ShapeDtypeStruct((3, RIM, SUBLANES, LANES), jnp.float32),
+        ),
+        in_specs=[VMEM] * 4,
+        out_specs=(HBM, VMEM),
+        scratch_shapes=[
+            pltpu.VMEM((3, seg + 2, SUBLANES, LANES), jnp.float32),
+            pltpu.VMEM((3, seg, SUBLANES, LANES), jnp.float32),
             pltpu.SemaphoreType.DMA((PIECES, 6)),
         ],
-        compiler_params=pltpu.CompilerParams(vmem_limit_bytes=32 * 2**20),
-        name="z_slopes_and_filter",
-    )(vel, local, xsums, jnp.asarray(line_table()), before_z, after_z)
+        compiler_params=pltpu.CompilerParams(vmem_limit_bytes=24 * 2**20),
+        cost_estimate=pl.CostEstimate(flops=20 * points, bytes_accessed=12 * points, transcendentals=0),
+        name="compact_filter",
+    )(terms, local, ups, downs)
 
 
 def rim_kernel(seg, o_in, rim_ref, vel_ref, xsums_ref, one_ref, two_ref, o_ref, edge, top, bottom, sems):
@@ -571,10 +631,11 @@
     before_z = lax.ppermute(numbers, "gz", forward)
     after_z = lax.ppermute(numbers, "gz", backward)
     local, xsums = x_part(vel, seg)
-    out, rim, one, two = z_part(vel, local, xsums, seg, before_z, after_z)
+    terms, ups, downs, one, two = z_part(vel, local, xsums, seg, before_z, after_z)
     first_swap, second_swap = pairs("gx")
     one = lax.ppermute(one, "gx", first_swap)
     two = lax.ppermute(two, "gx", second_swap)
+    out, rim = filter_part(terms, local, ups, downs, seg)
     return rim_part(out, rim, vel, xsums, one, two, seg).reshape(velocity.shape)
 
 

time: 39.4 us -> 34.1 us (0.87)
  waiting for transfers between devices: 3.33 us -> 0.01 us
  Pallas kernels: 27.5 us -> 26.4 us
  local copies, waits for them, and re-layouts: 0.84 us -> 0.01 us
    pallas_call x1, Pallas kernels: 16.7 us -> 9.57 us  [z_part(): pl.pallas_call(functools.partial(z_kernel, seg), out_shape=(jax.ShapeDtyp...]
    pallas_call x0 -> x1, Pallas kernels: none -> 6.02 us  [filter_part(): pl.pallas_call(functools.partial(filter_kernel, seg), out_shape=(jax.Shap...]
    ppermute x1, waiting for transfers between devices: 3.32 us -> 0.01 us  [blocked(): two = lax.ppermute(two, 'gx', second_swap)]
    unnamed x4 -> x2, local copies, waits for them, and re-layouts: 0.84 us -> 0.01 us
  transfers between devices with their start and end apart: 4 -> 4, of which waited for: 1 -> 0; matrix products, arithmetic and copies ran while one was open for 0% -> 0% of each run, Pallas kernels for 14% -> 34%
where the time goes in v1:
time: 34.1 us; the launch traced here: 33.9 us
  Pallas kernels  26.4 us (77%)
  starting transfers between devices  7.5 us (22%)
    pallas_call x1, Pallas kernels, z_part(): pl.pallas_call(functools.partial(z_kernel, seg), out_shape=(jax.ShapeDtyp...  9.57 us
    pallas_call x1, Pallas kernels, filter_part(): pl.pallas_call(functools.partial(filter_kernel, seg), out_shape=(jax.Shap...  6.02 us
    pallas_call x1, Pallas kernels, x_part(): pl.pallas_call(functools.partial(x_kernel, seg), out_shape=(jax.ShapeDtyp...  5.35 us
    pallas_call x1, Pallas kernels, ends(): pl.pallas_call(functools.partial(ends_kernel, seg), out_shape=(jax.ShapeD...  4.01 us
    ppermute x1, starting transfers between devices, blocked(): after_z = lax.ppermute(numbers, 'gz', backward)  3.39 us
    ppermute x1, starting transfers between devices, blocked(): two = lax.ppermute(two, 'gx', second_swap)  2.48 us
    ppermute x1, starting transfers between devices, blocked(): one = lax.ppermute(one, 'gx', first_swap)  1.63 us
    pallas_call x1, Pallas kernels, rim_part(): pl.pallas_call(functools.partial(rim_kernel, seg), out_shape=jax.ShapeDty...  1.42 us
  transfers between devices with their start and end apart: 4, of which 0 were waited for; matrix products, arithmetic and copies ran while one was open for 0% of the time, Pallas kernels for 34%

profile of v1, /device:TPU:0, one launch (start us, length us, event | category | flops | bytes accessed | tf_op | source)
XLA Modules:
  0.0 33.9 jit_solution(4426603719571041624)
XLA Ops:
  0.0 0.0 copy-start
  0.0 4.0 %line_ends.1 = (f32[3,512,8,128]{3,2,1,0:T(8,128)S(1)}, f32[24,1024]{1,0:T(8,128)S(1)}) custom-call(f32[3,2,512,4,128]{4,3,2,1,0:T(4,128)} %bitcast.2), custom_call_target="tpu_custom_call" | custom-call | tf_op jit(solution)/shard_map/line_ends/pallas_call | solution.py:163
  4.0 3.4 %collective-permute-start.1 = (f32[24,1024]{1,0:T(8,128)S(1)}, f32[24,1024]{1,0:T(8,128)S(1)}, u32[]{:S(2)}, u32[]{:S(2)}) collective-permute-start(f32[24,1024]{1,0:T(8,128)S(1)} %get-tuple-element.19), channel_id=1, source_target_pairs={{1,0},{2,1},{3,2},{4,3},{5,4},{6,5},{7,6},{0,7},{9,8},{10,9},{11,1... | collective-permute-start | bytes 294920 | tf_op jit(solution)/shard_map/ppermute | solution.py:632
  7.4 0.0 collective-permute-start
  7.4 5.4 %x_slopes.1 = (f32[3,512,8,128]{3,2,1,0:T(8,128)S(1)}, f32[2,6,8,128]{3,2,1,0:T(8,128)S(1)}) custom-call(f32[3,512,8,128]{3,2,1,0:T(8,128)S(1)} %get-tuple-element.16.vel_ref), custom_call_target="tpu_custom_call" | custom-call | flops 94371840 | bytes 12582912 | tf_op jit(solution)/shard_map/x_slopes/pallas_call | solution.py:226
  12.8 0.0 collective-permute-done.1.zr_ref
  12.8 0.0 collective-permute-done.zl_ref
  12.8 0.0 copy-done
  12.8 9.6 %z_slopes.1 = (f32[12288,128]{1,0:T(8,128)S(1)}, f32[3,8,128]{2,1,0:T(8,128)S(1)}, f32[3,8,128]{2,1,0:T(8,128)S(1)}, f32[20,4,128]{2,1,0:T(4,128)S(1)}, f32[20,4,128]{2,1,0:T(4,128)S(1)}) custom-call(f32[3,512,8,128]{3,2,1,0:T(8,128)S(1)} %get-tuple-element.16.vel_ref, f32[3,512,8,128]{3,2,1,0:T(8,128)S(1)} %get-tuple-element.17.sx_ref.x_ref, ...), custom_call_target="tpu_custom_call" | custom-call | tf_op jit(solution)/shard_map/z_slopes/pallas_call | solution.py:362
  22.4 1.6 %collective-permute-start.2 = (f32[20,4,128]{2,1,0:T(4,128)S(1)}, f32[20,4,128]{2,1,0:T(4,128)S(1)}, u32[]{:S(2)}, u32[]{:S(2)}) collective-permute-start(f32[20,4,128]{2,1,0:T(4,128)S(1)} %get-tuple-element.25), channel_id=1, source_target_pairs={{0,8},{8,0},{16,24},{24,16},{1,9},{9,1},{17,25},{25,17},{2,10},{10... | collective-permute-start | bytes 122888 | tf_op jit(solution)/shard_map/ppermute | solution.py:636
  24.0 2.5 %collective-permute-start.3 = (f32[20,4,128]{2,1,0:T(4,128)S(1)}, f32[20,4,128]{2,1,0:T(4,128)S(1)}, u32[]{:S(2)}, u32[]{:S(2)}) collective-permute-start(f32[20,4,128]{2,1,0:T(4,128)S(1)} %get-tuple-element.26), channel_id=1, source_target_pairs={{0,24},{8,16},{16,8},{24,0},{1,25},{9,17},{17,9},{25,1},{2,26},{10... | collective-permute-start | bytes 122888 | tf_op jit(solution)/shard_map/ppermute | solution.py:637
  26.5 6.0 %compact_filter.1 = (f32[3,2,512,4,128]{4,3,2,1,0:T(4,128)}, f32[3,128,8,128]{3,2,1,0:T(8,128)S(1)}) custom-call(f32[12288,128]{1,0:T(8,128)S(1)} %get-tuple-element.20.z_ref, f32[3,512,8,128]{3,2,1,0:T(8,128)S(1)} %get-tuple-element.17.sx_ref.x_ref, f32[3,8,128]{2,1,0:T(8,128)S(1)} %get-tuple-element.21.ups_ref, f32[3,8,128]{2,1,0:T(8,128)S(1)} %get-tuple-element.22.downs_ref), custom_call_target="tpu_custom_call" | custom-call | flops 31457280 | bytes 18874368 | tf_op jit(solution)/shard_map/compact_filter/pallas_call | solution.py:523
  32.5 0.0 collective-permute-done.2.one_ref
  32.5 0.0 collective-permute-done.3.two_ref
  32.5 1.4 %rim.1 = f32[3,2,512,4,128]{4,3,2,1,0:T(4,128)} custom-call(f32[3,2,512,4,128]{4,3,2,1,0:T(4,128)} %get-tuple-element.23.o_in, f32[3,128,8,128]{3,2,1,0:T(8,128)S(1)} %get-tuple-element.24.rim_ref, f32[3,512,8,128]{3,2,1,0:T(8,128)S(1)} %get-tuple-element.16.vel_ref, ...), custom_call_target="tpu_custom_call", output_to_operand_aliasing={{}: (0, {})} | custom-call | tf_op jit(solution)/shard_map/rim/pallas_call | solution.py:597
Async XLA Ops:
  0.0 12.8 %copy-start = (f32[256,128]{1,0:T(8,128)S(1)}, f32[256,128]{1,0:T(8,128)}, u32[]{:S(2)}) copy-start(f32[256,128]{1,0:T(8,128)} %constant.2.clone.table_ref) | copy-start | bytes 393220
  4.0 8.7 %collective-permute-start.1 = (f32[24,1024]{1,0:T(8,128)S(1)}, f32[24,1024]{1,0:T(8,128)S(1)}, u32[]{:S(2)}, u32[]{:S(2)}) collective-permute-start(f32[24,1024]{1,0:T(8,128)S(1)} %get-tuple-element.19), channel_id=1, source_target_pairs={{1,0},{2,1},{3,2},{4,3},{5,4},{6,5},{7,6},{0,7},{9,8},{10,9},{11,1... | collective-permute-start | bytes 294920 | tf_op jit(solution)/shard_map/ppermute | solution.py:632
  7.4 5.4 %collective-permute-start = (f32[24,1024]{1,0:T(8,128)S(1)}, f32[24,1024]{1,0:T(8,128)S(1)}, u32[]{:S(2)}, u32[]{:S(2)}) collective-permute-start(f32[24,1024]{1,0:T(8,128)S(1)} %get-tuple-element.19), channel_id=1, source_target_pairs={{0,1},{1,2},{2,3},{3,4},{4,5},{5,6},{6,7},{7,0},{8,9},{9,10},{10,1... | collective-permute-start | bytes 294920 | tf_op jit(solution)/shard_map/ppermute | solution.py:631
  22.4 10.1 %collective-permute-start.2 = (f32[20,4,128]{2,1,0:T(4,128)S(1)}, f32[20,4,128]{2,1,0:T(4,128)S(1)}, u32[]{:S(2)}, u32[]{:S(2)}) collective-permute-start(f32[20,4,128]{2,1,0:T(4,128)S(1)} %get-tuple-element.25), channel_id=1, source_target_pairs={{0,8},{8,0},{16,24},{24,16},{1,9},{9,1},{17,25},{25,17},{2,10},{10... | collective-permute-start | bytes 122888 | tf_op jit(solution)/shard_map/ppermute | solution.py:636
  24.0 8.5 %collective-permute-start.3 = (f32[20,4,128]{2,1,0:T(4,128)S(1)}, f32[20,4,128]{2,1,0:T(4,128)S(1)}, u32[]{:S(2)}, u32[]{:S(2)}) collective-permute-start(f32[20,4,128]{2,1,0:T(4,128)S(1)} %get-tuple-element.26), channel_id=1, source_target_pairs={{0,24},{8,16},{16,8},{24,0},{1,25},{9,17},{17,9},{25,1},{2,26},{10... | collective-permute-start | bytes 122888 | tf_op jit(solution)/shard_map/ppermute | solution.py:637

commit v2 on v1

--- a/solution.py
+++ b/solution.py
@@ -19,7 +19,7 @@
 REACH_D = 24
 REACH_F = 96
 RIM = 128
-STEP_ROWS = 64
+STEP_ROWS = 128
 PIECES = 4
 AHEAD = 4
 GROUP = 4
@@ -269,6 +269,7 @@
             halo_hi[field, at, :] = high
             halo_lo[field, at, :] = low
 
+    along_x = sx_ref.reshape(3 * seg * SUBLANES, LANES)
     low_lane = jnp.where(low_lanes(rows), 1.0, 0.0).astype(jnp.bfloat16) > 0.5
 
     def strided(c, xi, n):
@@ -315,7 +316,8 @@
                     for k in range(step_rows // 8):
                         at = (c * seg + xi + 8 * k) * SUBLANES + 4 * h + n
                         piece = h * (step_rows // 8) + k
-                        sbuf[pl.ds(at, 8, stride=SUBLANES), :] = term[piece * 8 : piece * 8 + 8]
+                        at = pl.ds(at, 8, stride=SUBLANES)
+                        sbuf[at, :] = term[piece * 8 : piece * 8 + 8] + along_x[at, :]
 
     zero = jnp.zeros((SUBLANES, LANES), jnp.float32)
 
@@ -327,7 +329,7 @@
 
     def row_of(c, row):
         at = pl.ds(pl.multiple_of((c * seg + row) * SUBLANES, SUBLANES), SUBLANES)
-        return sbuf[at, :] + sx_ref[c, row]
+        return sbuf[at, :]
 
     def sums_of(k, sums):
         ups, downs = sums
@@ -377,12 +379,12 @@
             pltpu.VMEM((6, 2 * seg, LANES), jnp.bfloat16),
             pltpu.VMEM((20, SUBLANES, LANES), jnp.float32),
         ],
-        compiler_params=pltpu.CompilerParams(vmem_limit_bytes=20 * 2**20),
+        compiler_params=pltpu.CompilerParams(vmem_limit_bytes=28 * 2**20),
         name="z_slopes",
     )(vel, local, xsums, jnp.asarray(line_table()), before_z, after_z)
 
 
-def filter_kernel(seg, z_ref, x_ref, ups_ref, downs_ref, o_ref, rim_ref, s_buf, o_buf, sems):
+def filter_kernel(seg, s_ref, ups_ref, downs_ref, o_ref, rim_ref, o_buf, sems):
     size = seg // PIECES
     turns = size // GROUP
     warm_group = REACH_F // turns
@@ -390,7 +392,7 @@
 
     def term(c, row):
         at = pl.ds(pl.multiple_of((c * seg + row) * SUBLANES, SUBLANES), SUBLANES)
-        return z_ref[at, :] + x_ref[c, row]
+        return s_ref[at, :]
 
     def to_second(value):
         return jnp.where(first, 0.0, pltpu.roll(value, 4, axis=0))
@@ -418,7 +420,6 @@
             results.append(found)
         for k in range(count):
             for c in range(3):
-                s_buf[c, low + k] = lines[k][c]
                 o_buf[c, low + k - 2] = results[k][c]
         return carry
 
@@ -432,7 +433,7 @@
     def up_rows(b, i, ups):
         low = (b + 1) * size - GROUP * (i + 1)
         order = list(reversed(range(GROUP)))
-        here = {(k, c): s_buf[c, low + k] for k in order for c in range(3)}
+        here = {(k, c): term(c, low + k) for k in order for c in range(3)}
         found = {(k, c): o_buf[c, low + k] for k in order for c in range(3)}
         for k in order:
             ups = tuple(here[k, c] + ROOT_F * ups[c] for c in range(3))
@@ -463,13 +464,7 @@
         for c in range(3)
     )
     for k in range(2):
-        here = [term(c, k) for c in range(3)]
-        for c in range(3):
-            s_buf[c, k] = here[c]
-        carry = down_row(here, carry)[1]
-    for c in range(3):
-        for k in range(2):
-            s_buf[c, seg + k] = to_first(s_buf[c, k])
+        carry = down_row([term(c, k) for c in range(3)], carry)[1]
     last = tuple(to_first(ups_ref[c]) for c in range(3))
 
     def opening(i, state):
@@ -491,19 +486,17 @@
                 carry, ups = state
                 return down_rows(b + 1, i, carry), up_rows(b, i, ups)
 
-            carry, _ = lax.fori_loop(0, turns - 1, body, (carry, warmed))
+            carry, _ = lax.fori_loop(0, turns - 1, body, (carry, warmed), unroll=4)
             _ = up_rows(b, turns - 1, _)
             low = seg - GROUP + 2
             for k in range(GROUP):
                 row = low + k
-                here = [term(c, row) if row < seg else s_buf[c, row] for c in range(3)]
+                here = [term(c, row) if row < seg else to_first(term(c, row - seg)) for c in range(3)]
                 found, carry = down_row(here, carry)
                 for c in range(3):
-                    if row < seg:
-                        s_buf[c, row] = here[c]
                     o_buf[c, row - 2] = found[c]
         else:
-            lax.fori_loop(0, turns, lambda i, ups: up_rows(PIECES - 1, i, ups), last)
+            lax.fori_loop(0, turns, lambda i, ups: up_rows(PIECES - 1, i, ups), last, unroll=4)
         for copy in store(b):
             copy.start()
 
@@ -518,7 +511,7 @@
             copy.wait()
 
 
-def filter_part(terms, local, ups, downs, seg):
+def filter_part(terms, ups, downs, seg):
     points = 3 * 2 * seg * 4 * LANES
     return pl.pallas_call(
         functools.partial(filter_kernel, seg),
@@ -526,17 +519,16 @@
             jax.ShapeDtypeStruct((3, 2, seg, 4, LANES), jnp.float32),
             jax.ShapeDtypeStruct((3, RIM, SUBLANES, LANES), jnp.float32),
         ),
-        in_specs=[VMEM] * 4,
+        in_specs=[VMEM] * 3,
         out_specs=(HBM, VMEM),
         scratch_shapes=[
-            pltpu.VMEM((3, seg + 2, SUBLANES, LANES), jnp.float32),
             pltpu.VMEM((3, seg, SUBLANES, LANES), jnp.float32),
             pltpu.SemaphoreType.DMA((PIECES, 6)),
         ],
         compiler_params=pltpu.CompilerParams(vmem_limit_bytes=24 * 2**20),
         cost_estimate=pl.CostEstimate(flops=20 * points, bytes_accessed=12 * points, transcendentals=0),
         name="compact_filter",
-    )(terms, local, ups, downs)
+    )(terms, ups, downs)
 
 
 def rim_kernel(seg, o_in, rim_ref, vel_ref, xsums_ref, one_ref, two_ref, o_ref, edge, top, bottom, sems):
@@ -635,7 +627,7 @@
     first_swap, second_swap = pairs("gx")
     one = lax.ppermute(one, "gx", first_swap)
     two = lax.ppermute(two, "gx", second_swap)
-    out, rim = filter_part(terms, local, ups, downs, seg)
+    out, rim = filter_part(terms, ups, downs, seg)
     return rim_part(out, rim, vel, xsums, one, two, seg).reshape(velocity.shape)
 
 

time: 34.1 us -> 32.6 us (0.956)
  Pallas kernels: 26.4 us -> 24.8 us
    pallas_call x1, Pallas kernels: 6.02 us -> 5.09 us  [filter_part(): pl.pallas_call(functools.partial(filter_kernel, seg), out_shape=(jax.Shap...]
    pallas_call x1, Pallas kernels: 9.57 us -> 8.97 us  [z_part(): pl.pallas_call(functools.partial(z_kernel, seg), out_shape=(jax.ShapeDtyp...]
  transfers between devices with their start and end apart: 4 -> 4, of which waited for: 0 -> 0; matrix products, arithmetic and copies ran while one was open for 0% -> 0% of each run, Pallas kernels for 34% -> 32%
where the time goes in v2:
time: 32.6 us; the launch traced here: 32.4 us
  Pallas kernels  24.8 us (76%)
  starting transfers between devices  7.5 us (23%)
    pallas_call x1, Pallas kernels, z_part(): pl.pallas_call(functools.partial(z_kernel, seg), out_shape=(jax.ShapeDtyp...  8.97 us
    pallas_call x1, Pallas kernels, x_part(): pl.pallas_call(functools.partial(x_kernel, seg), out_shape=(jax.ShapeDtyp...  5.35 us
    pallas_call x1, Pallas kernels, filter_part(): pl.pallas_call(functools.partial(filter_kernel, seg), out_shape=(jax.Shap...  5.09 us
    pallas_call x1, Pallas kernels, ends(): pl.pallas_call(functools.partial(ends_kernel, seg), out_shape=(jax.ShapeD...  4.01 us
    ppermute x1, starting transfers between devices, blocked(): after_z = lax.ppermute(numbers, 'gz', backward)  3.39 us
    ppermute x1, starting transfers between devices, blocked(): two = lax.ppermute(two, 'gx', second_swap)  2.48 us
    ppermute x1, starting transfers between devices, blocked(): one = lax.ppermute(one, 'gx', first_swap)  1.64 us
    pallas_call x1, Pallas kernels, rim_part(): pl.pallas_call(functools.partial(rim_kernel, seg), out_shape=jax.ShapeDty...  1.42 us
  transfers between devices with their start and end apart: 4, of which 0 were waited for; matrix products, arithmetic and copies ran while one was open for 0% of the time, Pallas kernels for 32%

profile of v2, /device:TPU:0, one launch (start us, length us, event | category | flops | bytes accessed | tf_op | source)
XLA Modules:
  0.0 32.4 jit_solution(11100642262103123788)
XLA Ops:
  0.0 0.0 copy-start
  0.0 4.0 %line_ends.1 = (f32[3,512,8,128]{3,2,1,0:T(8,128)S(1)}, f32[24,1024]{1,0:T(8,128)S(1)}) custom-call(f32[3,2,512,4,128]{4,3,2,1,0:T(4,128)} %bitcast.2), custom_call_target="tpu_custom_call" | custom-call | tf_op jit(solution)/shard_map/line_ends/pallas_call | solution.py:163
  4.0 3.4 %collective-permute-start.1 = (f32[24,1024]{1,0:T(8,128)S(1)}, f32[24,1024]{1,0:T(8,128)S(1)}, u32[]{:S(2)}, u32[]{:S(2)}) collective-permute-start(f32[24,1024]{1,0:T(8,128)S(1)} %get-tuple-element.19), channel_id=1, source_target_pairs={{1,0},{2,1},{3,2},{4,3},{5,4},{6,5},{7,6},{0,7},{9,8},{10,9},{11,1... | collective-permute-start | bytes 294920 | tf_op jit(solution)/shard_map/ppermute | solution.py:624
  7.4 0.0 collective-permute-start
  7.4 5.4 %x_slopes.1 = (f32[3,512,8,128]{3,2,1,0:T(8,128)S(1)}, f32[2,6,8,128]{3,2,1,0:T(8,128)S(1)}) custom-call(f32[3,512,8,128]{3,2,1,0:T(8,128)S(1)} %get-tuple-element.16.vel_ref), custom_call_target="tpu_custom_call" | custom-call | flops 94371840 | bytes 12582912 | tf_op jit(solution)/shard_map/x_slopes/pallas_call | solution.py:226
  12.8 0.0 collective-permute-done.1.zr_ref
  12.8 0.0 collective-permute-done.zl_ref
  12.8 0.0 copy-done
  12.8 9.0 %z_slopes.1 = (f32[12288,128]{1,0:T(8,128)S(1)}, f32[3,8,128]{2,1,0:T(8,128)S(1)}, f32[3,8,128]{2,1,0:T(8,128)S(1)}, f32[20,4,128]{2,1,0:T(4,128)S(1)}, f32[20,4,128]{2,1,0:T(4,128)S(1)}) custom-call(f32[3,512,8,128]{3,2,1,0:T(8,128)S(1)} %get-tuple-element.16.vel_ref, f32[3,512,8,128]{3,2,1,0:T(8,128)S(1)} %get-tuple-element.17.sx_ref, ...), custom_call_target="tpu_custom_call" | custom-call | tf_op jit(solution)/shard_map/z_slopes/pallas_call | solution.py:364
  21.8 1.6 %collective-permute-start.2 = (f32[20,4,128]{2,1,0:T(4,128)S(1)}, f32[20,4,128]{2,1,0:T(4,128)S(1)}, u32[]{:S(2)}, u32[]{:S(2)}) collective-permute-start(f32[20,4,128]{2,1,0:T(4,128)S(1)} %get-tuple-element.25), channel_id=1, source_target_pairs={{0,8},{8,0},{16,24},{24,16},{1,9},{9,1},{17,25},{25,17},{2,10},{10... | collective-permute-start | bytes 122888 | tf_op jit(solution)/shard_map/ppermute | solution.py:628
  23.4 2.5 %collective-permute-start.3 = (f32[20,4,128]{2,1,0:T(4,128)S(1)}, f32[20,4,128]{2,1,0:T(4,128)S(1)}, u32[]{:S(2)}, u32[]{:S(2)}) collective-permute-start(f32[20,4,128]{2,1,0:T(4,128)S(1)} %get-tuple-element.26), channel_id=1, source_target_pairs={{0,24},{8,16},{16,8},{24,0},{1,25},{9,17},{17,9},{25,1},{2,26},{10... | collective-permute-start | bytes 122888 | tf_op jit(solution)/shard_map/ppermute | solution.py:629
  25.9 5.1 %compact_filter.1 = (f32[3,2,512,4,128]{4,3,2,1,0:T(4,128)}, f32[3,128,8,128]{3,2,1,0:T(8,128)S(1)}) custom-call(f32[12288,128]{1,0:T(8,128)S(1)} %get-tuple-element.20.s_ref, f32[3,8,128]{2,1,0:T(8,128)S(1)} %get-tuple-element.21.ups_ref, f32[3,8,128]{2,1,0:T(8,128)S(1)} %get-tuple-element.22.downs_ref), custom_call_target="tpu_custom_call" | custom-call | flops 31457280 | bytes 18874368 | tf_op jit(solution)/shard_map/compact_filter/pallas_call | solution.py:516
  31.0 0.0 collective-permute-done.2.one_ref
  31.0 0.0 collective-permute-done.3.two_ref
  31.0 1.4 %rim.1 = f32[3,2,512,4,128]{4,3,2,1,0:T(4,128)} custom-call(f32[3,2,512,4,128]{4,3,2,1,0:T(4,128)} %get-tuple-element.23.o_in, f32[3,128,8,128]{3,2,1,0:T(8,128)S(1)} %get-tuple-element.24.rim_ref, f32[3,512,8,128]{3,2,1,0:T(8,128)S(1)} %get-tuple-element.16.vel_ref, ...), custom_call_target="tpu_custom_call", output_to_operand_aliasing={{}: (0, {})} | custom-call | tf_op jit(solution)/shard_map/rim/pallas_call | solution.py:589
Async XLA Ops:
  0.0 12.8 %copy-start = (f32[256,128]{1,0:T(8,128)S(1)}, f32[256,128]{1,0:T(8,128)}, u32[]{:S(2)}) copy-start(f32[256,128]{1,0:T(8,128)} %constant.2.clone.table_ref) | copy-start | bytes 393220
  4.0 8.7 %collective-permute-start.1 = (f32[24,1024]{1,0:T(8,128)S(1)}, f32[24,1024]{1,0:T(8,128)S(1)}, u32[]{:S(2)}, u32[]{:S(2)}) collective-permute-start(f32[24,1024]{1,0:T(8,128)S(1)} %get-tuple-element.19), channel_id=1, source_target_pairs={{1,0},{2,1},{3,2},{4,3},{5,4},{6,5},{7,6},{0,7},{9,8},{10,9},{11,1... | collective-permute-start | bytes 294920 | tf_op jit(solution)/shard_map/ppermute | solution.py:624
  7.4 5.4 %collective-permute-start = (f32[24,1024]{1,0:T(8,128)S(1)}, f32[24,1024]{1,0:T(8,128)S(1)}, u32[]{:S(2)}, u32[]{:S(2)}) collective-permute-start(f32[24,1024]{1,0:T(8,128)S(1)} %get-tuple-element.19), channel_id=1, source_target_pairs={{0,1},{1,2},{2,3},{3,4},{4,5},{5,6},{6,7},{7,0},{8,9},{9,10},{10,1... | collective-permute-start | bytes 294920 | tf_op jit(solution)/shard_map/ppermute | solution.py:623
  21.8 9.2 %collective-permute-start.2 = (f32[20,4,128]{2,1,0:T(4,128)S(1)}, f32[20,4,128]{2,1,0:T(4,128)S(1)}, u32[]{:S(2)}, u32[]{:S(2)}) collective-permute-start(f32[20,4,128]{2,1,0:T(4,128)S(1)} %get-tuple-element.25), channel_id=1, source_target_pairs={{0,8},{8,0},{16,24},{24,16},{1,9},{9,1},{17,25},{25,17},{2,10},{10... | collective-permute-start | bytes 122888 | tf_op jit(solution)/shard_map/ppermute | solution.py:628
  23.4 7.6 %collective-permute-start.3 = (f32[20,4,128]{2,1,0:T(4,128)S(1)}, f32[20,4,128]{2,1,0:T(4,128)S(1)}, u32[]{:S(2)}, u32[]{:S(2)}) collective-permute-start(f32[20,4,128]{2,1,0:T(4,128)S(1)} %get-tuple-element.26), channel_id=1, source_target_pairs={{0,24},{8,16},{16,8},{24,0},{1,25},{9,17},{17,9},{25,1},{2,26},{10... | collective-permute-start | bytes 122888 | tf_op jit(solution)/shard_map/ppermute | solution.py:629

commit v3 on v2

--- a/solution.py
+++ b/solution.py
@@ -212,11 +212,11 @@
         return carry
 
     carry = lax.fori_loop(0, reach, lambda i, k: advance(other(seg - reach + i, False), k)[1], start, unroll=8)
-    carry = lax.fori_loop(0, seg, forward, carry, unroll=16)
+    carry = lax.fori_loop(0, seg, forward, carry, unroll=32)
     for field in range(6):
         sums_ref[0, field] = carry[0][field]
     carry = lax.fori_loop(0, reach, lambda i, k: advance(other(reach - 1 - i, True), k)[1], start, unroll=8)
-    carry = lax.fori_loop(0, seg, backward, carry, unroll=16)
+    carry = lax.fori_loop(0, seg, backward, carry, unroll=32)
     for field in range(6):
         sums_ref[1, field] = carry[0][field]
 

time: 32.6 us -> 32.5 us (level)
  no operation moved by 1% of the time
where the time goes in v3:
time: 32.5 us; the launch traced here: 32.3 us
  Pallas kernels  24.8 us (76%)
  starting transfers between devices  7.5 us (23%)
    pallas_call x1, Pallas kernels, z_part(): pl.pallas_call(functools.partial(z_kernel, seg), out_shape=(jax.ShapeDtyp...  8.97 us
    pallas_call x1, Pallas kernels, x_part(): pl.pallas_call(functools.partial(x_kernel, seg), out_shape=(jax.ShapeDtyp...  5.28 us
    pallas_call x1, Pallas kernels, filter_part(): pl.pallas_call(functools.partial(filter_kernel, seg), out_shape=(jax.Shap...  5.09 us
    pallas_call x1, Pallas kernels, ends(): pl.pallas_call(functools.partial(ends_kernel, seg), out_shape=(jax.ShapeD...  4.01 us
    ppermute x1, starting transfers between devices, blocked(): after_z = lax.ppermute(numbers, 'gz', backward)  3.39 us
    ppermute x1, starting transfers between devices, blocked(): two = lax.ppermute(two, 'gx', second_swap)  2.48 us
    ppermute x1, starting transfers between devices, blocked(): one = lax.ppermute(one, 'gx', first_swap)  1.64 us
    pallas_call x1, Pallas kernels, rim_part(): pl.pallas_call(functools.partial(rim_kernel, seg), out_shape=jax.ShapeDty...  1.42 us
  transfers between devices with their start and end apart: 4, of which 0 were waited for; matrix products, arithmetic and copies ran while one was open for 0% of the time, Pallas kernels for 32%

profile of v3, /device:TPU:0, one launch (start us, length us, event | category | flops | bytes accessed | tf_op | source)
XLA Modules:
  0.0 32.3 jit_solution(1990018097296072528)
XLA Ops:
  0.0 0.0 copy-start
  0.0 4.0 %line_ends.1 = (f32[3,512,8,128]{3,2,1,0:T(8,128)S(1)}, f32[24,1024]{1,0:T(8,128)S(1)}) custom-call(f32[3,2,512,4,128]{4,3,2,1,0:T(4,128)} %bitcast.2), custom_call_target="tpu_custom_call" | custom-call | tf_op jit(solution)/shard_map/line_ends/pallas_call | solution.py:163
  4.0 3.4 %collective-permute-start.1 = (f32[24,1024]{1,0:T(8,128)S(1)}, f32[24,1024]{1,0:T(8,128)S(1)}, u32[]{:S(2)}, u32[]{:S(2)}) collective-permute-start(f32[24,1024]{1,0:T(8,128)S(1)} %get-tuple-element.19), channel_id=1, source_target_pairs={{1,0},{2,1},{3,2},{4,3},{5,4},{6,5},{7,6},{0,7},{9,8},{10,9},{11,1... | collective-permute-start | bytes 294920 | tf_op jit(solution)/shard_map/ppermute | solution.py:624
  7.4 0.0 collective-permute-start
  7.4 5.3 %x_slopes.1 = (f32[3,512,8,128]{3,2,1,0:T(8,128)S(1)}, f32[2,6,8,128]{3,2,1,0:T(8,128)S(1)}) custom-call(f32[3,512,8,128]{3,2,1,0:T(8,128)S(1)} %get-tuple-element.16.vel_ref), custom_call_target="tpu_custom_call" | custom-call | flops 94371840 | bytes 12582912 | tf_op jit(solution)/shard_map/x_slopes/pallas_call | solution.py:226
  12.7 0.0 collective-permute-done.1.zr_ref
  12.7 0.0 collective-permute-done.zl_ref
  12.7 0.0 copy-done
  12.7 9.0 %z_slopes.1 = (f32[12288,128]{1,0:T(8,128)S(1)}, f32[3,8,128]{2,1,0:T(8,128)S(1)}, f32[3,8,128]{2,1,0:T(8,128)S(1)}, f32[20,4,128]{2,1,0:T(4,128)S(1)}, f32[20,4,128]{2,1,0:T(4,128)S(1)}) custom-call(f32[3,512,8,128]{3,2,1,0:T(8,128)S(1)} %get-tuple-element.16.vel_ref, f32[3,512,8,128]{3,2,1,0:T(8,128)S(1)} %get-tuple-element.17.sx_ref, ...), custom_call_target="tpu_custom_call" | custom-call | tf_op jit(solution)/shard_map/z_slopes/pallas_call | solution.py:364
  21.7 1.6 %collective-permute-start.2 = (f32[20,4,128]{2,1,0:T(4,128)S(1)}, f32[20,4,128]{2,1,0:T(4,128)S(1)}, u32[]{:S(2)}, u32[]{:S(2)}) collective-permute-start(f32[20,4,128]{2,1,0:T(4,128)S(1)} %get-tuple-element.25), channel_id=1, source_target_pairs={{0,8},{8,0},{16,24},{24,16},{1,9},{9,1},{17,25},{25,17},{2,10},{10... | collective-permute-start | bytes 122888 | tf_op jit(solution)/shard_map/ppermute | solution.py:628
  23.3 2.5 %collective-permute-start.3 = (f32[20,4,128]{2,1,0:T(4,128)S(1)}, f32[20,4,128]{2,1,0:T(4,128)S(1)}, u32[]{:S(2)}, u32[]{:S(2)}) collective-permute-start(f32[20,4,128]{2,1,0:T(4,128)S(1)} %get-tuple-element.26), channel_id=1, source_target_pairs={{0,24},{8,16},{16,8},{24,0},{1,25},{9,17},{17,9},{25,1},{2,26},{10... | collective-permute-start | bytes 122888 | tf_op jit(solution)/shard_map/ppermute | solution.py:629
  25.8 5.1 %compact_filter.1 = (f32[3,2,512,4,128]{4,3,2,1,0:T(4,128)}, f32[3,128,8,128]{3,2,1,0:T(8,128)S(1)}) custom-call(f32[12288,128]{1,0:T(8,128)S(1)} %get-tuple-element.20.s_ref, f32[3,8,128]{2,1,0:T(8,128)S(1)} %get-tuple-element.21.ups_ref, f32[3,8,128]{2,1,0:T(8,128)S(1)} %get-tuple-element.22.downs_ref), custom_call_target="tpu_custom_call" | custom-call | flops 31457280 | bytes 18874368 | tf_op jit(solution)/shard_map/compact_filter/pallas_call | solution.py:516
  30.9 0.0 collective-permute-done.2.one_ref
  30.9 0.0 collective-permute-done.3.two_ref
  30.9 1.4 %rim.1 = f32[3,2,512,4,128]{4,3,2,1,0:T(4,128)} custom-call(f32[3,2,512,4,128]{4,3,2,1,0:T(4,128)} %get-tuple-element.23.o_in, f32[3,128,8,128]{3,2,1,0:T(8,128)S(1)} %get-tuple-element.24.rim_ref, f32[3,512,8,128]{3,2,1,0:T(8,128)S(1)} %get-tuple-element.16.vel_ref, ...), custom_call_target="tpu_custom_call", output_to_operand_aliasing={{}: (0, {})} | custom-call | tf_op jit(solution)/shard_map/rim/pallas_call | solution.py:589
Async XLA Ops:
  0.0 12.7 %copy-start = (f32[256,128]{1,0:T(8,128)S(1)}, f32[256,128]{1,0:T(8,128)}, u32[]{:S(2)}) copy-start(f32[256,128]{1,0:T(8,128)} %constant.2.clone.table_ref) | copy-start | bytes 393220
  4.0 8.7 %collective-permute-start.1 = (f32[24,1024]{1,0:T(8,128)S(1)}, f32[24,1024]{1,0:T(8,128)S(1)}, u32[]{:S(2)}, u32[]{:S(2)}) collective-permute-start(f32[24,1024]{1,0:T(8,128)S(1)} %get-tuple-element.19), channel_id=1, source_target_pairs={{1,0},{2,1},{3,2},{4,3},{5,4},{6,5},{7,6},{0,7},{9,8},{10,9},{11,1... | collective-permute-start | bytes 294920 | tf_op jit(solution)/shard_map/ppermute | solution.py:624
  7.4 5.3 %collective-permute-start = (f32[24,1024]{1,0:T(8,128)S(1)}, f32[24,1024]{1,0:T(8,128)S(1)}, u32[]{:S(2)}, u32[]{:S(2)}) collective-permute-start(f32[24,1024]{1,0:T(8,128)S(1)} %get-tuple-element.19), channel_id=1, source_target_pairs={{0,1},{1,2},{2,3},{3,4},{4,5},{5,6},{6,7},{7,0},{8,9},{9,10},{10,1... | collective-permute-start | bytes 294920 | tf_op jit(solution)/shard_map/ppermute | solution.py:623
  21.7 9.2 %collective-permute-start.2 = (f32[20,4,128]{2,1,0:T(4,128)S(1)}, f32[20,4,128]{2,1,0:T(4,128)S(1)}, u32[]{:S(2)}, u32[]{:S(2)}) collective-permute-start(f32[20,4,128]{2,1,0:T(4,128)S(1)} %get-tuple-element.25), channel_id=1, source_target_pairs={{0,8},{8,0},{16,24},{24,16},{1,9},{9,1},{17,25},{25,17},{2,10},{10... | collective-permute-start | bytes 122888 | tf_op jit(solution)/shard_map/ppermute | solution.py:628
  23.3 7.6 %collective-permute-start.3 = (f32[20,4,128]{2,1,0:T(4,128)S(1)}, f32[20,4,128]{2,1,0:T(4,128)S(1)}, u32[]{:S(2)}, u32[]{:S(2)}) collective-permute-start(f32[20,4,128]{2,1,0:T(4,128)S(1)} %get-tuple-element.26), channel_id=1, source_target_pairs={{0,24},{8,16},{16,8},{24,0},{1,25},{9,17},{17,9},{25,1},{2,26},{10... | collective-permute-start | bytes 122888 | tf_op jit(solution)/shard_map/ppermute | solution.py:629
